TPU v7x, 32 devices: a whole 2x2x4 slice. The times are simulated.
32 devices in a mesh: wide: 16 (over z, x, core), narrow: 2 (over y).
Axes of the slice: x: 2, y: 2, z: 4, core: 2. Of those that a mesh axis runs over, the one named last changes fastest.
Arguments:
- tokens: bfloat16 [32768, 768], P(('wide', 'narrow')), may hold values from -6 to 6
- patch_grid: int32 [64, 4, 2], P(('wide', 'narrow')), may hold values from 8 to 11
- qkv_rows: bfloat16 [13824, 128], P(('wide', 'narrow')), may hold values from -0.21875 to 0.21875
- proj_rows: bfloat16 [4608, 128], P(('wide', 'narrow')), may hold values from -0.625 to 0.625
- fc1_rows: bfloat16 [18432, 128], P(('wide', 'narrow')), may hold values from -0.21875 to 0.21875
- fc2_rows: bfloat16 [18432, 128], P(('wide', 'narrow')), may hold values from -0.15625 to 0.15625
- norm_gain: float32 [2, 768], replicated, may hold values from 0.5 to 1.5
- norm_bias: float32 [2, 768], replicated, may hold values from -2 to 2
- qv_bias: float32 [2, 768], replicated, may hold values from -2 to 2
- proj_bias: float32 [768], replicated, may hold values from -2 to 2
- fc1_bias: float32 [3072], replicated, may hold values from -2 to 2
- fc2_bias: float32 [768], replicated, may hold values from -2 to 2
- layer_scale: float32 [2, 768], replicated, may hold values from 0.1 to 0.4
- cotangent: bfloat16 [32768, 768], P(('wide', 'narrow')), may hold values from -6 to 6
Outputs:
- layer_out: bfloat16 [32768, 768], P(('wide', 'narrow'))
- input_grad: float32 [32768, 768], P(('wide', 'narrow'))
- qkv_grad: float32 [13824, 128], P(('wide', 'narrow'))
- proj_grad: float32 [4608, 128], P(('wide', 'narrow'))
- fc1_grad: float32 [18432, 128], P(('wide', 'narrow'))
- fc2_grad: float32 [18432, 128], P(('wide', 'narrow'))
- gain_grad: float32 [2, 768], replicated
- norm_bias_grad: float32 [2, 768], replicated
- qv_bias_grad: float32 [2, 768], replicated
- proj_bias_grad: float32 [768], replicated
- fc1_bias_grad: float32 [3072], replicated
- fc2_bias_grad: float32 [768], replicated
- scale_grad: float32 [2, 768], replicated
All inputs are finite; a program needn't handle non-finite values.
Results may differ from a plain program's by a relative error of at most 0.0087.
Values may be sent and summed in bfloat16 or wider, within the bound.
No kernel may reach another device: no remote copies, remote signals or barrier semaphores. Data moves between devices by JAX's collectives and lax.ppermute only.
A program may use at most 192 MiB of HBM per device.

v0:
```python
from functools import partial

import jax
import jax.numpy as jnp
from jax import lax
from jax.experimental import pallas as pl
from jax.experimental.pallas import tpu as pltpu
from jax.sharding import PartitionSpec as P

H = 12
PREFIX = 5
EPSILON = 1e-06
NEGATIVE = -1e30
AXES = ("wide", "narrow")
COLUMNS = 8
BF16 = jnp.bfloat16
F32 = jnp.float32


def dot(a, b):
    return lax.dot_general(a, b, (((1,), (0,)), ((), ())), preferred_element_type=F32)


def dot_nt(a, b):
    return lax.dot_general(a, b, (((1,), (1,)), ((), ())), preferred_element_type=F32)


def dot_tn(a, b):
    return lax.dot_general(a, b, (((0,), (0,)), ((), ())), preferred_element_type=F32)


TOKEN = (8, 128)


def call(kernel, grid, scalars, ins, outs, scratch=(), after=(), mib=36, alias=None):
    n, m = len(scalars) + len(ins), len(outs)

    def run(*refs):
        rest = refs[n + len(after) :]
        rest[m][...] = jnp.zeros(TOKEN, F32)
        kernel(*refs[:n], *rest[:m], *rest[m + 1 :])

    anywhere = pl.BlockSpec(memory_space=pl.ANY)
    return pl.pallas_call(
        run,
        grid_spec=pltpu.PrefetchScalarGridSpec(
            num_scalar_prefetch=len(scalars),
            grid=grid,
            in_specs=[spec for _, spec in ins] + [anywhere] * len(after),
            out_specs=[out[2] for out in outs] + [full(TOKEN)],
            scratch_shapes=list(scratch),
        ),
        out_shape=[
            pltpu.HBM(out[0], out[1]) if len(out) > 3 else jax.ShapeDtypeStruct(out[0], out[1]) for out in outs
        ]
        + [jax.ShapeDtypeStruct(TOKEN, F32)],
        input_output_aliases={n + k: to for k, to in (alias or {}).items()},
        compiler_params=pltpu.CompilerParams(vmem_limit_bytes=mib * 2**20),
        cost_estimate=pl.CostEstimate(flops=1, bytes_accessed=1, transcendentals=0),
    )(*scalars, *(array for array, _ in ins), *after)


def far(v):
    return pltpu.with_memory_space_constraint(v, pltpu.HBM)


def full(shape):
    return pl.BlockSpec(shape, lambda *_: (0,) * len(shape), pipeline_mode=pl.Buffered(1))


def standardize(v):
    centered = v - jnp.mean(v, axis=-1, keepdims=True)
    inverse = lax.rsqrt(jnp.mean(centered * centered, axis=-1, keepdims=True) + EPSILON)
    return centered * inverse, inverse


def standardize_back(grad, scaled, inverse):
    return inverse * (
        grad
        - jnp.mean(grad, axis=-1, keepdims=True)
        - scaled * jnp.mean(grad * scaled, axis=-1, keepdims=True)
    )


def length_of(grid_ref, image):
    return PREFIX + grid_ref[2 * image] * grid_ref[2 * image + 1]


def spans(grid_ref, pack, images):
    found, start = [], 0
    for i in range(images):
        length = length_of(grid_ref, pack * images + i)
        found.append((start, length))
        start = start + length
    return found


def join(scr, core, own, other):
    for i in range(scr.shape[0]):
        scr[i, core] = own[i]
        scr[i, 1 - core] = other[i]
    blocks, cores, rows, columns = scr.shape
    return scr[...].reshape(blocks * cores * rows, columns)


def part(core, matrix, own, other):
    blocks, rows, columns = own.shape
    cut = matrix.reshape(blocks, 2, rows, columns)
    own[...] = jnp.where(core == 0, cut[:, 0], cut[:, 1])
    other[...] = jnp.where(core == 0, cut[:, 1], cut[:, 0])


def prepare_kernel(grid_ref, tok, cot, gain, bias, ls, x, n1, up, b2g, sums, *, images):
    pack = pl.program_id(0)
    slot = tok.shape[0] // images
    row = lax.broadcasted_iota(jnp.int32, (slot, tok.shape[0]), 0)
    column = lax.broadcasted_iota(jnp.int32, (slot, tok.shape[0]), 1)

    def image(i, carry):
        start, total = carry
        length = length_of(grid_ref, pack * images + i)
        place = jnp.where((column - row == start) & (row < length), 1.0, 0.0).astype(BF16)
        rows = pl.ds(pl.multiple_of(i * slot, slot), slot)
        moved = dot(place, tok[...])
        x[rows] = moved.astype(BF16)
        scaled, _ = standardize(moved)
        n1[rows] = (scaled * gain[0:1] + bias[0:1]).astype(BF16)
        upstream = dot(place, cot[...])
        up[rows] = upstream.astype(BF16)
        low = (ls[1:2] * upstream).astype(BF16)
        b2g[rows] = low
        return start + length, total + column_sum(low.astype(F32))

    _, total = lax.fori_loop(0, images, image, (jnp.int32(0), jnp.zeros((1, tok.shape[1]), F32)))

    @pl.when(pack == 0)
    def _():
        sums[...] = jnp.zeros_like(sums)

    sums[...] += total


def unplace(grid_ref, pack, images, size):
    slot = size // images
    row = lax.broadcasted_iota(jnp.int32, (size, slot), 0)
    column = lax.broadcasted_iota(jnp.int32, (size, slot), 1)
    return jnp.concatenate(
        [
            jnp.where((row - column == start) & (column < length), 1.0, 0.0).astype(BF16)
            for start, length in spans(grid_ref, pack, images)
        ],
        axis=1,
    )


def pieces(rows, size=128):
    return [pl.ds(r, size) for r in range(0, rows, size)]


def eights(v):
    return jnp.sum(v.reshape(-1, 8, v.shape[1]), axis=0)


def column_sum(v):
    return jnp.sum(v, axis=0, keepdims=True)


def stacked(v, low):
    zero = jnp.zeros_like(v)
    return jnp.concatenate([jnp.where(low, v, zero), jnp.where(low, zero, v)], axis=0)


def attend_kernel(grid_ref, sc, n1, own, other, offset, proj, att, log_total, scr, *, slot, head):
    step = pl.program_id(0)
    width = n1.shape[1]
    per = n1.shape[0] // slot
    pair = 2 * head
    heads = width // head

    @pl.when(step == 0)
    def _():
        join(scr, sc[0], own, other)

    w = scr[...].reshape(width, 3 * width)
    proj[...] = (dot(n1[...], w) + offset[...]).astype(BF16)
    low = lax.broadcasted_iota(jnp.int32, (slot, pair), 1) < head
    key_at = lax.broadcasted_iota(jnp.int32, (slot, slot), 0)
    for i in range(per):
        ok = key_at < length_of(grid_ref, step * per + i)
        rows = pl.ds(i * slot, slot)
        found = []
        for j in range(width // pair):
            q, k = (proj[rows, pl.ds(t * width + j * pair, pair)] for t in range(2))
            scores = dot_nt(stacked(k, low), q * jnp.asarray(head ** (-0.5), BF16))
            halves = []
            for h in range(2):
                masked = jnp.where(ok, scores[h * slot : (h + 1) * slot], NEGATIVE)
                top = jnp.max(masked, axis=0, keepdims=True)
                exponent = jnp.exp(masked - top)
                total = column_sum(exponent)
                halves.append((exponent * (1.0 / total)).astype(BF16))
                log_total[pl.ds(i * heads + 2 * j + h, 1)] = top + jnp.log(total)
            found.append(jnp.concatenate(halves, axis=0))
        for j, p in enumerate(found):
            v = proj[rows, pl.ds(2 * width + j * pair, pair)]
            att[rows, pl.ds(j * pair, pair)] = dot_tn(p, stacked(v, low)).astype(BF16)


def middle_kernel(sc, att, x, gain, bias, ls, proj_bias, own, other, b1, n2, acc, scr):
    acc[...] = dot(att[...], join(scr, sc[0], own, other))
    for rows in pieces(acc.shape[0]):
        branch = acc[rows] + proj_bias[...]
        b1[rows] = branch
        scaled, _ = standardize(x[rows].astype(F32) + ls[0:1] * branch)
        n2[rows] = (scaled * gain[1:2] + bias[1:2]).astype(BF16)


def hidden_kernel(sc, n2, b2g, fc1_bias, own, other, act, slope, go, gs, scr):
    w1 = join(scr, sc[0], own, other)
    for rows in pieces(n2.shape[0], 256):
        hidden = dot(n2[rows], w1) + fc1_bias[...]
        normal = 0.5 * (1.0 + lax.erf(hidden * 0.5**0.5))
        act[rows] = (hidden * normal).astype(BF16)
        density = (0.5 / jnp.pi) ** 0.5 * jnp.exp(-0.5 * hidden * hidden)
        slope[rows] = normal + hidden * density
    part(sc[0], dot_tn(act[...], b2g[...]).astype(BF16), go, gs)


def hidden_back_kernel(sc, b2g, n2, slope, own, other, hg, sums, go, gs, n2t, scr):
    @pl.when(pl.program_id(0) == 0)
    def _():
        n2t[...] = n2[...].T

    w2 = join(scr, sc[0], own, other)
    total = jnp.zeros((8, sums.shape[1]), F32)
    for rows in pieces(b2g.shape[0], 256):
        low = (dot_nt(b2g[rows], w2) * slope[rows]).astype(BF16)
        hg[rows] = low
        total = total + eights(low.astype(F32))
    sums[...] = column_sum(total)
    part(sc[0], dot(n2t[...], hg[...]).astype(BF16), go, gs)


def middle_back_kernel(sc, hg, own, other, po, ps, b1, x, up, gain, ls, mg, b1g, ag, sums, acc, scr, pscr, *, tiles):
    step = pl.program_id(0)

    @pl.when(step == 0)
    def _():
        acc[...] = jnp.zeros_like(acc)

    @pl.when(step < tiles)
    def _():
        acc[...] += dot_nt(hg[...], join(scr, sc[0], own, other))

    @pl.when(step == tiles)
    def _():
        join(pscr, sc[0], po, ps)
        sums[...] = jnp.zeros_like(sums)

    @pl.when(step >= tiles)
    def _():
        size = x.shape[0]
        totals = [jnp.zeros((8, x.shape[1]), F32) for _ in range(4)]
        for rows in pieces(size):
            branch = b1[rows]
            scaled, inverse = standardize(x[rows].astype(F32) + ls[0:1] * branch)
            grad = acc[pl.ds(pl.multiple_of((step - tiles) * size + rows.start, 128), rows.size)]
            back = up[rows].astype(F32) + standardize_back(grad * gain[1:2], scaled, inverse)
            mg[rows] = back
            low = (ls[0:1] * back).astype(BF16)
            b1g[rows] = low
            terms = (back * branch, low.astype(F32), grad * scaled, grad)
            totals = [t + eights(v) for t, v in zip(totals, terms)]
        ag[...] = dot_nt(b1g[...], pscr[...].reshape(x.shape[1], x.shape[1])).astype(BF16)
        sums[...] += jnp.concatenate([column_sum(t) for t in totals], axis=0)


def attend_back_kernel(grid_ref, proj, ag, log_total, pg, sums, *, slot, head):
    step = pl.program_id(0)
    width = ag.shape[1]
    per = ag.shape[0] // slot
    pair = 2 * head
    heads = width // head
    factor = head ** (-0.5)
    low = lax.broadcasted_iota(jnp.int32, (slot, pair), 1) < head
    key_at = lax.broadcasted_iota(jnp.int32, (slot, slot), 0)

    @pl.when(step == 0)
    def _():
        sums[...] = jnp.zeros_like(sums)

    for i in range(per):
        ok = key_at < length_of(grid_ref, step * per + i)
        rows = pl.ds(i * slot, slot)
        found = []

        def put(t, j, d):
            d = d.astype(BF16)
            columns = pl.ds(t * width + j * pair, pair)
            pg[rows, columns] = d
            if t != 1:
                sums[:, columns] += eights(d.astype(F32))

        for j in range(width // pair):
            q, k, v = (proj[rows, pl.ds(t * width + j * pair, pair)] for t in range(3))
            out = ag[rows, pl.ds(j * pair, pair)]
            q = q * jnp.asarray(factor, BF16)
            k2 = stacked(k, low)
            scores = dot_nt(k2, q)
            pull = dot_nt(stacked(v, low), out)
            ps, ss = [], []
            for h in range(2):
                half = slice(h * slot, (h + 1) * slot)
                p = jnp.exp(jnp.where(ok, scores[half], NEGATIVE) - log_total[pl.ds(i * heads + 2 * j + h, 1)])
                g = pull[half]
                ps.append(p.astype(BF16))
                ss.append((p * (g - column_sum(g * p))).astype(BF16))
            s = jnp.concatenate(ss, axis=0)
            dk = dot(s, q)
            dv = dot(jnp.concatenate(ps, axis=0), out)
            put(1, j, jnp.where(low, dk[:slot], dk[slot:]))
            put(2, j, jnp.where(low, dv[:slot], dv[slot:]))
            found.append((s, k2))
        for j, (s, k2) in enumerate(found):
            put(0, j, dot_tn(s, k2) * factor)


def weight_kernel(sc, n1, att, pg, b1g, go, gs, n1t):
    step = pl.program_id(0)
    last = pl.num_programs(0) - 1

    @pl.when(step == 0)
    def _():
        n1t[...] = n1[...].T

    @pl.when(step < last)
    def _():
        part(sc[0], dot(n1t[...], pg[...]).astype(BF16), go, gs)

    @pl.when(step == last)
    def _():
        part(sc[0], dot_tn(att[...], b1g[...]).astype(BF16), go, gs)


def input_back_kernel(grid_ref, sc, pg, own, other, x, mg, gain, out, sums, scr, acc, high, mid, *, images):
    pack = pl.program_id(0)

    @pl.when(pack == 0)
    def _():
        join(scr, sc[0], own, other)
        sums[...] = jnp.zeros_like(sums)

    width = x.shape[1]
    acc[...] = dot_nt(pg[...], scr[...].reshape(width, 3 * width))
    totals = [jnp.zeros((8, width), F32) for _ in range(2)]
    for rows in pieces(acc.shape[0]):
        grad = acc[rows]
        scaled, inverse = standardize(x[rows].astype(F32))
        back = mg[rows] + standardize_back(grad * gain[0:1], scaled, inverse)
        totals = [t + eights(v) for t, v in zip(totals, (grad * scaled, grad))]
        big = back.astype(BF16)
        high[rows] = big
        mid[rows] = (back - big.astype(F32)).astype(BF16)
    sums[...] += jnp.concatenate([column_sum(t) for t in totals], axis=0)
    place = unplace(grid_ref, pack, images, x.shape[0])
    out[...] = dot(place, high[...]) + dot(place, mid[...])


def layer_out_kernel(grid_ref, sc, act, own, other, x, b1, up, ls, fc2_bias, out, sums, acc, result, scr, *, images, tiles):
    step = pl.program_id(0)

    @pl.when(step == 0)
    def _():
        acc[...] = jnp.zeros_like(acc)

    @pl.when(step < tiles)
    def _():
        acc[...] += dot(act[...], join(scr, sc[0], own, other))

    @pl.when(step == tiles)
    def _():
        sums[...] = jnp.zeros_like(sums)

    @pl.when(step >= tiles)
    def _():
        pack, size = step - tiles, out.shape[0]
        total = jnp.zeros((8, x.shape[1]), F32)
        for rows in pieces(size):
            branch = acc[pl.ds(pl.multiple_of(pack * size + rows.start, 128), rows.size)] + fc2_bias[...]
            total = total + eights(up[rows].astype(F32) * branch)
            middle = x[rows].astype(F32) + ls[0:1] * b1[rows]
            result[rows] = (middle + ls[1:2] * branch).astype(BF16)
        out[...] = dot(unplace(grid_ref, pack, images, size), result[...]).astype(BF16)
        sums[...] += column_sum(total)


Y, CORE, X, Z = 1, 2, 4, 8


def swap(v, mask):
    return lax.ppermute(v, AXES, [(i, i ^ mask) for i in range(32)])


def move(plan, sc, ins, outs, after, mib=8):
    def kernel(*refs):
        for a, b in plan(*refs):
            b[...] = a[...]

    return call(
        kernel, (1,), (sc,), [(v, full(v.shape)) for v in ins], [(shape, BF16, full(shape)) for shape in outs], (), after, mib
    )


def gather_line(block):
    return [block] + [swap(block, Z * k) for k in (1, 2, 3)]


def gather_stack(line, sc, after, sides=()):
    rows, columns = line[0].shape
    half = columns // 2
    shapes = [(4, rows, half)] * 2 + [(2, 2) + side.shape for side in sides[:1]]

    def plan(sc, *refs):
        ins, outs = refs[: 4 + len(sides)], refs[4 + len(sides) :]
        pairs = [(ins[k].at[:, pl.ds(h * half, half)], outs[h].at[k]) for k in range(4) for h in range(2)]
        return pairs + [(side, outs[2].at[i // 2, i % 2]) for i, side in enumerate(ins[4:])]

    return move(plan, sc, [*line, *sides], shapes, after)


def gather_columns(line, sc, after):
    _, _, rows, half = line[0].shape

    def plan(sc, *refs):
        return [(refs[k].at[h, i], refs[4 + h].at[i, k]) for k in range(4) for h in range(2) for i in range(2)]

    return move(plan, sc, line, [(2, 4, rows, half)] * 2, after)


def pack_rows(qkv, proj, fc1, fc2, width, tiles):
    arrays = (qkv, proj, fc1, fc2)
    rows = proj.shape[0] * 128 // width
    columns = [v.shape[0] * 128 // rows for v in arrays]
    places = [(0, 0), (0, columns[0]), (1, 0), (2, 0)]
    half = columns[3] // 2

    def kernel(*refs):
        ins, outs, scrs = refs[:4], refs[4:8], refs[8:]
        for n, (ref, scr) in enumerate(zip(ins, scrs)):
            scr[...] = ref[...].astype(F32)
            if n < 3:
                blocks = [(i, columns[n] // 128) for i in range(columns[n] // 128)]
            else:
                lanes = width // 128
                blocks = [(k * rows * lanes + i, lanes) for k in range(tiles) for i in range(lanes)]
            for i, (start, stride) in enumerate(blocks):
                to, at = places[n]
                at += i * 128
                if n == 3:
                    to, at = to + at // half, at % half
                outs[to][:, pl.ds(at, 128)] = scr[pl.ds(start, rows, stride=stride)].astype(BF16)

    shapes = [(rows, columns[0] + columns[1]), (rows, columns[2]), (rows, half), (rows, half)]
    scratch = [pltpu.VMEM(v.shape, F32) for v in arrays]
    outs = [(shape, BF16, full(shape)) for shape in shapes]
    return call(kernel, (1,), (), [(v, full(v.shape)) for v in arrays], outs, scratch, (), mib=8)[:4]


def gather_pair(a, b, sc, after):
    def plan(sc, a, xa, b, yb, left, right):
        return [(a, left.at[0]), (xa, left.at[1]), (b, right.at[0]), (yb, right.at[1])]

    return move(plan, sc, (a, swap(a, X), b, swap(b, Y)), [(2,) + a.shape] * 2, after)


def gather_place(left, right, sc, after, runs=1):
    _, _, rows, half = left.shape
    width = 2 * half // runs

    def plan(sc, left, other_left, right, other_right, out):
        pairs = []
        for n, sides in enumerate(((left, other_left), (right, other_right))):
            for i in range(2):
                for j in range(2):
                    for k in range(4):
                        x, y = (i, j) if n == 0 else (j, i)
                        to = out.at[sc[3] ^ k, sc[1] ^ x, sc[2] ^ y]
                        if runs == 1:
                            pairs.append((sides[j].at[i, k], to.at[:, pl.ds(n * half, half)]))
                            continue
                        for r in range(runs // 2):
                            run = n * (runs // 2) + r
                            pairs.append((sides[j].at[i, k, :, pl.ds(r * width, width)], to.at[pl.ds(run * rows, rows)]))
        return pairs

    ins = [far(v) for v in (left, swap(left, Y), right, swap(right, X))]
    own, token = move(plan, sc, ins, [(4, 2, 2, runs * rows, width)], after, 12)
    shape = (COLUMNS, 2 * runs * rows, width)
    return own.reshape(shape), swap(own, CORE).reshape(shape), token


def add(a, b):
    return a.astype(F32) + b.astype(F32)


def fold_core(own, other, sc, after):
    _, rows2, columns = own.shape
    rows, half = rows2 // 2, columns // 2
    by_z = pl.BlockSpec((1, 2, 2, rows, columns), lambda i, *_: (i, 0, 0, 0, 0))
    to_z = pl.BlockSpec((1, 2, rows, half), lambda i, *_: (i, 0, 0, 0))
    left, right = pl.ds(0, half), pl.ds(half, half)

    def kernel(sc, own, got, ka, sa, kb, sb):
        for i in range(2):
            for a, b, flip in ((ka, kb, 0), (sa, sb, 1)):
                y, x = sc[2] ^ flip, sc[1] ^ flip
                a[0, i] = add(own[0, i, y, :, left], got[0, i, y, :, left]).astype(BF16)
                b[0, i] = add(own[0, x, i, :, right], got[0, x, i, :, right]).astype(BF16)

    ins = [(v.reshape(4, 2, 2, rows, columns), by_z) for v in (own, swap(other, CORE))]
    ka, sa, kb, sb, token = call(kernel, (4,), (sc,), ins, [((4, 2, rows, half), BF16, to_z)] * 4, (), after, mib=12)
    return [(ka, sa, Y), (kb, sb, X)], token


def columns_of(parts):
    rows = min(keep.shape[2] for keep, _, _ in parts)
    places, at = [], 0
    for n, (keep, _, _) in enumerate(parts):
        for first in range(0, keep.shape[2], rows):
            places.append((n, first, at, keep.shape[3]))
            at += keep.shape[3]
    return rows, at, places


def fold_first(parts, sc, after):
    groups = [[part for part in parts if part[2] == mask] for mask in (Y, X)]
    ins = [(v, full(v.shape)) for group in groups for keep, send, mask in group for v in (keep, swap(send, mask))]
    layouts = [columns_of(group) for group in groups]
    outs = [((4, rows, width), BF16, full((4, rows, width))) for rows, width, _ in layouts for _ in range(2)]

    def kernel(sc, *refs):
        ins, outs, base = refs[: len(ins_)], refs[len(ins_) :], 0
        for g, (rows, _, places) in enumerate(layouts):
            for n, first, at, width in places:
                keep, got = ins[base + 2 * n], ins[base + 2 * n + 1]
                cut = pl.ds(first, rows)
                for z in range(4):
                    for flip in range(2):
                        here = sc[1 + g] ^ flip
                        to = outs[2 * g + flip]
                        to[z, :, pl.ds(at, width)] = add(keep[z, here, cut], got[z, here, cut]).astype(BF16)
            base += 2 * len(groups[g])

    ins_ = ins
    out = call(kernel, (1,), (sc,), ins, outs, (), after, mib=16)
    return [(out[0], out[1], X), (out[2], out[3], Y)], out[4]


def fold_second(parts, sc, after):
    ins = [(v, full(v.shape)) for keep, send, mask in parts for v in (keep, swap(send, mask))]
    _, rows, width = parts[0][0].shape
    shape = (rows, 2 * width)

    def kernel(sc, *refs):
        ins, outs = refs[:4], refs[4:]
        for k, to in enumerate(outs):
            z = sc[3] ^ k
            for n in range(2):
                to[:, pl.ds(n * width, width)] = add(ins[2 * n][z], ins[2 * n + 1][z]).astype(to.dtype)

    outs = [(shape, F32, full(shape))] + [(shape, BF16, full(shape))] * 3
    return call(kernel, (1,), (sc,), ins, outs, (), after, mib=12)


def fold_sends(parts):
    keep, *sends, token = parts
    return token, [keep] + [swap(v, Z * k) for k, v in zip((1, 2, 3), sends)]


def fold_last(parts, shapes, runs, after):
    def kernel(keep, r1, r2, r3, *outs):
        rows = keep.shape[0]
        for i, (n, first, stride) in enumerate(runs):
            cut = (slice(None), pl.ds(i * 128, 128))
            total = keep[cut] + (r1[cut].astype(F32) + r2[cut].astype(F32) + r3[cut].astype(F32))
            outs[n][pl.ds(first, rows, stride=stride)] = total

    ins = [(v, full(v.shape)) for v in parts]
    return call(kernel, (1,), (), ins, [(shape, F32, full(shape)) for shape in shapes], (), after, mib=12)


def reduce_sends(v, masks):
    return [v] + [swap(v, mask) for mask in masks]


def reduce_level(ins, at, sc, after, split=None):
    v = ins[0]
    shapes, where = split or ([v.shape], [(0, pl.ds(i, 1)) for i in range(v.shape[0])])

    def kernel(sc, *refs):
        line, outs = refs[-1], refs[-1 - len(shapes) : -1]
        mine = sc[at[0]]
        for k in at[1:]:
            mine = 2 * mine + sc[k]
        for k, ref in enumerate(refs[: len(ins)]):
            line[mine ^ k] = ref[...]
        total = line[0]
        for k in range(1, len(ins)):
            total = total + line[k]
        for i, (n, place) in enumerate(where):
            row = total[i : i + 1]
            outs[n][place] = row[0] if len(shapes[n]) == 1 else row

    outs = [(shape, F32, full(shape)) for shape in shapes]
    scratch = [pltpu.VMEM((len(ins),) + v.shape, F32)]
    return call(kernel, (1,), (sc,), [(u, full(v.shape)) for u in ins], outs, scratch, after, mib=8)


def body(
    tokens,
    patch_grid,
    qkv_rows,
    proj_rows,
    fc1_rows,
    fc2_rows,
    norm_gain,
    norm_bias,
    qv_bias,
    proj_bias,
    fc1_bias,
    fc2_bias,
    layer_scale,
    cotangent,
):
    rows, width = tokens.shape
    packs, images, _ = patch_grid.shape
    pack = rows // packs
    slot = pack // images
    head = width // H
    hidden = fc1_bias.shape[0]
    row_width = qkv_rows.shape[1]
    tiles = hidden // width
    tile = min(256, rows)
    swaps = lax.axis_size("wide") == 16 and lax.axis_size("narrow") == 2
    if swaps:
        me = lax.axis_index(AXES)
        sc = jnp.stack([me // CORE % 2, me // X % 2, me % 2, me // Z]).astype(jnp.int32)
    else:
        sc = jnp.zeros((4,), jnp.int32)
    grid_flat = patch_grid.reshape(-1)
    thin, wide_rows = width // (2 * COLUMNS), hidden // (2 * COLUMNS)
    per_tile = COLUMNS // tiles

    by_pack = pl.BlockSpec((pack, width), lambda i, *_: (i, 0))
    by_tile = lambda w: pl.BlockSpec((tile, w), lambda i, *_: (i, 0))
    whole = full((rows, width))
    proj_blocks = pl.BlockSpec((COLUMNS, thin, width), lambda i, *_: (0, 0, 3), pipeline_mode=pl.Buffered(1))
    fc2_blocks = pl.BlockSpec((per_tile, wide_rows, width), lambda i, *_: (i, 0, 0))
    column_blocks = pl.BlockSpec((COLUMNS, thin, width), lambda i, *_: (0, 0, i))
    hidden_tile = pl.BlockSpec((rows, width), lambda i, *_: (0, i))
    vec1, vec2 = full((1, width)), full((2, width))
    hidden_vec = pl.BlockSpec((1, width), lambda i, *_: (0, i))
    qkv_blocks = full((COLUMNS, thin, 3 * width))
    qkv_scr = pltpu.VMEM((COLUMNS, 2, thin, 3 * width), BF16)
    fc2_scr = pltpu.VMEM((per_tile, 2, wide_rows, width), BF16)
    thin_scr = pltpu.VMEM((COLUMNS, 2, thin, width), BF16)
    sum_scr = pltpu.VMEM((rows, width), F32)
    turned_scr = pltpu.VMEM((width, rows), BF16)
    log_block = pl.BlockSpec((tile // slot * H, slot), lambda i, *_: (i, 0))

    halves = lambda v: v.reshape(COLUMNS, 2, -1, v.shape[1]).transpose(1, 0, 2, 3)
    ready = []
    if swaps:
        qp_block, fc1_block, a, b = pack_rows(qkv_rows, proj_rows, fc1_rows, fc2_rows, width, tiles)
        qp_line, fc1_line = gather_line(qp_block), gather_line(fc1_block)
        *qp_ab, message, _ = gather_stack(qp_line, sc, [], (a, swap(a, X), b, swap(b, Y)))
        fc2_line = gather_line(message)
        *qp_pair, token = gather_pair(*qp_ab, sc, [fc1_line[1], fc1_line[3]])
        ready = [token]
    else:
        qp_block = jnp.concatenate([qkv_rows.reshape(-1, 3 * width), proj_rows.reshape(-1, width)], axis=1)
        fc1_block, fc2_block = fc1_rows.reshape(-1, hidden), fc2_rows.reshape(-1, width)
        qp_own, qp_other = halves(lax.all_gather(qp_block, AXES, axis=0, tiled=True))
        fc1_own, fc1_other = halves(lax.all_gather(fc1_block, AXES, axis=0, tiled=True))
        fc2_own, fc2_other = halves(lax.all_gather(fc2_block, AXES, axis=0, tiled=True))

    x, n1, up, b2g, fc2_sums, token = call(
        partial(prepare_kernel, images=images),
        (packs,),
        (grid_flat,),
        [(far(tokens), by_pack), (far(cotangent), by_pack), (norm_gain, vec2), (norm_bias, vec2), (layer_scale, vec2)],
        [((rows, width), BF16, by_pack, "far")] * 4 + [((1, width), F32, vec1)],
        (),
        ready,
        mib=14,
    )

    ready = []
    if swaps:
        *fc1_ab, token = gather_stack(fc1_line, sc, [token, fc2_line[1]])
        qp_own, qp_other, token = gather_place(*qp_pair, sc, [token])
        ready = [token]

    offset = jnp.concatenate([qv_bias[0], jnp.zeros_like(qv_bias[0]), qv_bias[1]])[None]
    proj, att, log_total, token = call(
        partial(attend_kernel, slot=slot, head=head),
        (rows // tile,),
        (grid_flat, sc),
        [(far(n1), by_tile(width)), (qp_own, qkv_blocks), (qp_other, qkv_blocks), (offset, full((1, 3 * width)))],
        [((rows, 3 * width), BF16, by_tile(3 * width), "far"), ((rows, width), BF16, by_tile(width))]
        + [((rows // slot * H, slot), F32, log_block)],
        [qkv_scr],
        ready,
        mib=24,
    )
    ready = []
    if swaps:
        *fc1_pair, token = gather_pair(*fc1_ab, sc, [token, fc2_line[2]])
        ready = [token]
    b1, n2, token = call(
        middle_kernel,
        (1,),
        (sc,),
        [(att, whole), (x, whole), (norm_gain, vec2), (norm_bias, vec2), (layer_scale, vec2), (proj_bias[None], vec1)]
        + [(qp_own, proj_blocks), (qp_other, proj_blocks)],
        [((rows, width), F32, whole, "far"), ((rows, width), BF16, whole)],
        [sum_scr, thin_scr],
        ready,
        mib=20,
    )
    ready = []
    if swaps:
        *fc2_pair, token = gather_columns(fc2_line, sc, [token])
        fc1_own, fc1_other, token = gather_place(*fc1_pair, sc, [token])
        ready = [token]
    cut = tiles - 1

    def some_tiles(first, count, after, alias=None):
        columns = pl.BlockSpec((COLUMNS, thin, width), lambda i, *_: (0, 0, i + first))
        outs = pl.BlockSpec((rows, width), lambda i, *_: (0, i + first))
        blocks = pl.BlockSpec((per_tile, wide_rows, width), lambda i, *_: (i + first, 0, 0))
        return call(
            hidden_kernel,
            (count,),
            (sc,),
            [(n2, whole), (b2g, whole), (fc1_bias[None], pl.BlockSpec((1, width), lambda i, *_: (0, i + first)))]
            + [(fc1_own, columns), (fc1_other, columns)],
            [((rows, hidden), BF16, outs, "far"), ((rows, hidden), F32, outs, "far")]
            + [((COLUMNS, wide_rows, width), BF16, blocks, "far")] * 2,
            [thin_scr],
            after,
            mib=24,
            alias=alias,
        )

    *made, token = some_tiles(0, cut, ready)
    if swaps:
        fc2_own, fc2_other, token = gather_place(*fc2_pair, sc, [token], tiles)
    *made, token = some_tiles(cut, tiles - cut, made + [token], {i: i for i in range(4)})
    act, slope, fc2g_own, fc2g_other = made

    hg, fc1_sums, fc1g_own, fc1g_other, token = call(
        hidden_back_kernel,
        (tiles,),
        (sc,),
        [(far(b2g), whole), (far(n2), whole), (far(slope), hidden_tile), (fc2_own, fc2_blocks), (fc2_other, fc2_blocks)],
        [((rows, hidden), BF16, hidden_tile, "far"), ((1, hidden), F32, hidden_vec)]
        + [((COLUMNS, thin, hidden), BF16, column_blocks, "far")] * 2,
        [turned_scr, fc2_scr],
        mib=28,
    )
    chain = []
    if swaps:
        fc2_parts, token = fold_core(fc2g_own, fc2g_other, sc, [token])
        chain = [token]

    bound = lambda i: jnp.minimum(i, tiles - 1)
    hidden_first = pl.BlockSpec((rows, width), lambda i, *_: (0, bound(i)))
    column_first = pl.BlockSpec((COLUMNS, thin, width), lambda i, *_: (0, 0, bound(i)))
    fc2_first = pl.BlockSpec((per_tile, wide_rows, width), lambda i, *_: (bound(i), 0, 0))
    then = lambda size: pl.BlockSpec((size, width), lambda i, *_: (jnp.maximum(i - tiles, 0), 0))
    mg, b1g, ag, middle_sums, token = call(
        partial(middle_back_kernel, tiles=tiles),
        (tiles + rows // tile,),
        (sc,),
        [(far(hg), hidden_first), (fc1_own, column_first), (fc1_other, column_first)]
        + [(qp_own, proj_blocks), (qp_other, proj_blocks)]
        + [(b1, then(tile)), (x, then(tile)), (up, then(tile)), (norm_gain, vec2), (layer_scale, vec2)],
        [((rows, width), F32, then(tile), "far"), ((rows, width), BF16, then(tile)), ((rows, width), BF16, then(tile))]
        + [((4, width), F32, full((4, width)))],
        [sum_scr, thin_scr, thin_scr],
        chain,
        mib=28,
    )
    chain = []
    if swaps:
        fc1_parts, token = fold_core(fc1g_own, fc1g_other, sc, [token])
        chain = [token]

    pg, proj_sums, token = call(
        partial(attend_back_kernel, slot=slot, head=head),
        (rows // tile,),
        (grid_flat,),
        [(far(proj), by_tile(3 * width)), (ag, by_tile(width)), (log_total, log_block)],
        [((rows, 3 * width), BF16, by_tile(3 * width)), ((8, 3 * width), F32, full((8, 3 * width)))],
        (),
        chain,
        mib=14,
    )
    chain = []
    if swaps:
        fc_parts, token = fold_first(fc1_parts + fc2_parts, sc, [token])
        chain = [token]

    qp_grad_own, qp_grad_other, token = call(
        weight_kernel,
        (4,),
        (sc,),
        [(n1, whole), (att, whole), (pg, pl.BlockSpec((rows, width), lambda i, *_: (0, jnp.minimum(i, 2)))), (b1g, whole)],
        [((COLUMNS, thin, 4 * width), BF16, column_blocks)] * 2,
        [turned_scr],
        chain,
        mib=18,
    )
    layer_out, out_sums, token = call(
        partial(layer_out_kernel, images=images, tiles=tiles),
        (tiles + packs,),
        (grid_flat, sc),
        [(far(act), hidden_first), (fc2_own, fc2_first), (fc2_other, fc2_first), (x, then(pack)), (b1, then(pack)), (up, then(pack))]
        + [(layer_scale, vec2), (fc2_bias[None], vec1)],
        [((rows, width), BF16, then(pack), "far"), ((1, width), F32, vec1)],
        [sum_scr, pltpu.VMEM((pack, width), BF16), fc2_scr],
        [token],
        mib=26,
    )
    chain = []
    if swaps:
        qp_parts, token = fold_core(qp_grad_own, qp_grad_other, sc, [token])
        token, fc_parts = fold_sends(fold_second(fc_parts, sc, [token]))
        chain = [token]

    input_grad, input_sums, token = call(
        partial(input_back_kernel, images=images),
        (packs,),
        (grid_flat, sc),
        [(pg, pl.BlockSpec((pack, 3 * width), lambda i, *_: (i, 0))), (qp_own, qkv_blocks), (qp_other, qkv_blocks)]
        + [(x, by_pack), (mg, by_pack), (norm_gain, vec2)],
        [((rows, width), F32, by_pack, "far"), ((2, width), F32, vec2)],
        [qkv_scr, pltpu.VMEM((pack, width), F32)] + [pltpu.VMEM((pack, width), BF16)] * 2,
        chain,
        mib=26,
    )

    chain = []
    if swaps:
        qp_parts, token = fold_first(qp_parts, sc, [token, fc_parts[1], fc_parts[3]])
        chain = [token]

    def gather_sums(input_sums, middle, proj, fc2, out, fc1, to):
        q, v = column_sum(proj[:, pl.ds(0, width)]), column_sum(proj[:, pl.ds(2 * width, width)])
        lines = (input_sums[0:1], middle[2:3], input_sums[1:2], middle[3:4], q, v, middle[1:2], fc2[...], middle[0:1], out[...])
        for i, line in enumerate(lines):
            to[pl.ds(i, 1)] = line
        for i in range(tiles):
            to[pl.ds(len(lines) + i, 1)] = fc1[:, pl.ds(i * width, width)]

    sums_in = (input_sums, middle_sums, proj_sums, fc2_sums, out_sums, fc1_sums)
    sums, token = call(
        gather_sums,
        (1,),
        (),
        [(v, full(v.shape)) for v in sums_in],
        [((10 + tiles, width), F32, full((10 + tiles, width)))],
        (),
        chain,
    )
    if swaps:
        fc2_rows_of = fc2_rows.shape[0] // tiles
        n1_runs, n2_runs = hidden // 256, width // 256
        fc_runs = []
        for half in range(2):
            fc_runs += [(0, half * n1_runs + i, hidden // 128) for i in range(n1_runs)]
            fc_runs += [(1, k * fc2_rows_of + half * n2_runs + i, width // 128) for k in range(tiles) for i in range(n2_runs)]
        sums, token = reduce_level(reduce_sends(sums, (CORE,)), (0,), sc, [token])
        sums, token = reduce_level(reduce_sends(sums, (Y,)), (2,), sc, [token])
        token, qp_parts = fold_sends(fold_second(qp_parts, sc, [token, fc_parts[2]]))
        sums, token = reduce_level(reduce_sends(sums, (X,)), (1,), sc, [token])
        fc1_grad, fc2_grad, token = fold_last(fc_parts, (fc1_rows.shape, fc2_rows.shape), fc_runs, [token, qp_parts[1]])
        line = lambda i: pl.ds(i * width, width)
        shapes = [(2, width)] * 3 + [(width,), (hidden,), (width,), (2, width)]
        where = [(i // 2, pl.ds(i % 2, 1)) for i in range(6)] + [(3, line(0)), (5, line(0))]
        where += [(6, pl.ds(0, 1)), (6, pl.ds(1, 1))] + [(4, line(i)) for i in range(tiles)]
        sums = reduce_sends(sums, (Z, 2 * Z, 3 * Z))
        *small, token = reduce_level(sums, (3,), sc, [token] + qp_parts[2:], (shapes, where))
        qkv_runs, proj_runs = 3 * width // 128, width // 128
        qp_runs = [(0, i, qkv_runs) for i in range(qkv_runs)] + [(1, i, proj_runs) for i in range(proj_runs)]
        qkv_grad, proj_grad, _ = fold_last(qp_parts, (qkv_rows.shape, proj_rows.shape), qp_runs, [token])
    else:

        def scatter(own, other):
            matrix = jnp.stack([own, other], axis=1).reshape(-1, own.shape[-1])
            return lax.psum_scatter(matrix, AXES, scatter_dimension=0, tiled=True).astype(F32)

        fc2_grad = scatter(fc2g_own, fc2g_other).reshape(-1, row_width)
        fc1_grad = scatter(fc1g_own, fc1g_other).reshape(-1, row_width)
        qp_grad = scatter(qp_grad_own, qp_grad_other)
        qkv_grad = qp_grad[:, : 3 * width].reshape(-1, row_width)
        proj_grad = qp_grad[:, 3 * width :].reshape(-1, row_width)
        sums = lax.psum(sums, AXES)
        small = [sums[0:2], sums[2:4], sums[4:6], sums[6], sums[10:].reshape(-1), sums[7], sums[8:10]]
    return (
        layer_out,
        input_grad,
        qkv_grad,
        proj_grad,
        fc1_grad,
        fc2_grad,
        *(v.reshape(leaf.shape) for v, leaf in zip(small, (norm_gain, norm_bias, qv_bias, proj_bias, fc1_bias, fc2_bias, layer_scale))),
    )


def solution(mesh):
    split = P(AXES, None)
    return jax.shard_map(
        body,
        mesh=mesh,
        in_specs=(split, P(AXES, None, None)) + (split,) * 4 + (P(),) * 7 + (split,),
        out_specs=(split,) * 6 + (P(),) * 7,
        check_vma=False,
    )
```

profile of v0, /device:TPU:0, one launch (start us, length us, event | category | flops | bytes accessed | tf_op | source)
XLA Modules:
  0.0 249.5 jit_solution(10803903024535211727)
XLA Ops:
  4.7 3.0 %collective-permute-start = (bf16[24,3072]{1,0:T(8,128)(2,1)S(1)}, bf16[24,3072]{1,0:T(8,128)(2,1)S(1)}, u32[]{:S(2)}, u32[]{:S(2)}) collective-permute-start(bf16[24,3072]{1,0:T(8,128)(2,1)S(1)} %get-tuple-element.138.refs_1_), channel_id=1, source_target_pairs={{0,8},{1,9},{2,10},{3,11},{4,12},{5,13},{6,14},{7,15},{8,0},{9,1},... | collective-permute-start | bytes 442376 | tf_op jit(solution)/shard_map/ppermute | solution.py:401
  7.8 2.6 %collective-permute-start.1 = (bf16[24,3072]{1,0:T(8,128)(2,1)S(1)}, bf16[24,3072]{1,0:T(8,128)(2,1)S(1)}, u32[]{:S(2)}, u32[]{:S(2)}) collective-permute-start(bf16[24,3072]{1,0:T(8,128)(2,1)S(1)} %get-tuple-element.138.refs_1_), channel_id=1, source_target_pairs={{0,16},{1,17},{2,18},{3,19},{4,20},{5,21},{6,22},{7,23},{8,24},{9,... | collective-permute-start | bytes 442376 | tf_op jit(solution)/shard_map/ppermute | solution.py:401
  16.4 5.3 %collective-permute-done.1.refs_3_ = bf16[24,3072]{1,0:T(8,128)(2,1)S(1)} collective-permute-done((bf16[24,3072]{1,0:T(8,128)(2,1)S(1)}, bf16[24,3072]{1,0:T(8,128)(2,1)S(1)}, u32[]{:S(2)}, u32[]{:S(2)}) %collective-permute-start.1) | collective-permute-done | bytes 147488 | tf_op jit(solution)/shard_map/ppermute | solution.py:401
  28.3 2.5 collective-permute-start.8
  32.7 3.2 %collective-permute-done.8.refs_6_.refs_4_ = bf16[24,3072]{1,0:T(8,128)(2,1)S(1)} collective-permute-done((bf16[24,3072]{1,0:T(8,128)(2,1)S(1)}, bf16[24,3072]{1,0:T(8,128)(2,1)S(1)}, u32[]{:S(2)}, u32[]{:S(2)}) %collective-permute-start.8) | collective-permute-done | bytes 147488 | tf_op jit(solution)/shard_map/ppermute | solution.py:401
  37.7 2.6 %collective-permute-start.11 = (bf16[24,3072]{1,0:T(8,128)(2,1)S(1)}, bf16[24,3072]{1,0:T(8,128)(2,1)S(1)}, u32[]{:S(2)}, u32[]{:S(2)}) collective-permute-start(bf16[24,3072]{1,0:T(8,128)(2,1)S(1)} %get-tuple-element.143.refs_1_), channel_id=1, source_target_pairs={{0,16},{1,17},{2,18},{3,19},{4,20},{5,21},{6,22},{7,23},{8,24},{9,... | collective-permute-start | bytes 442376 | tf_op jit(solution)/shard_map/ppermute | solution.py:401
  40.5 7.7 %shard_map.240 = (bf16[1024,768]{1,0:T(8,128)(2,1)}, bf16[1024,768]{1,0:T(8,128)(2,1)}, bf16[1024,768]{1,0:T(8,128)(2,1)}, bf16[1024,768]{1,0:T(8,128)(2,1)}, f3...) custom-call(s32[16]{0:T(128)S(1)} %reshape.65.refs_0_, bf16[1024,768]{1,0:T(8,128)(2,1)} %refs_1_.3, bf16[1024,768]{1,0:T(8,128)(2,1)} %refs_2_.3, ...), custom_call_target="tpu_custom_call" | custom-call | flops 1 | bytes 1 | tf_op jit(solution)/shard_map/pallas_call | solution.py:44
  49.8 2.3 shard_map.242
  56.7 10.5 %shard_map.243 = (bf16[1024,2304]{1,0:T(8,128)(2,1)}, bf16[1024,768]{1,0:T(8,128)(2,1)S(1)}, f32[96,128]{1,0:T(8,128)S(1)}, f32[8,128]{1,0:T(8,128)S(1)}) custom-call(s32[16]{0:T(128)S(1)} %reshape.65.refs_0_, s32[4]{0:T(128)S(1)} %pad_add_fusion.refs_0_.refs_1_, bf16[1024,768]{1,0:T(8,128)(2,1)} %get-tuple-element.145.refs_2_.refs_1_, ...), custom_call_target="tpu_custom_call" | custom-call | flops 1 | bytes 1 | tf_op jit(solution)/shard_map/pallas_call | solution.py:44
  73.7 4.3 %shard_map.245 = (f32[1024,768]{1,0:T(8,128)}, bf16[1024,768]{1,0:T(8,128)(2,1)S(1)}, f32[8,128]{1,0:T(8,128)S(1)}) custom-call(s32[4]{0:T(128)S(1)} %pad_add_fusion.refs_0_.refs_1_, bf16[1024,768]{1,0:T(8,128)(2,1)S(1)} %get-tuple-element.153.refs_1_.refs_2_, bf16[1024,768]{1,0:T(8,128)(2,1)S(1)} %copy-done, f32[2,768]{1,0:T(2,128)S(1)} %copy-done.19, ...), custom_call_target="tpu_custom_call" | custom-call | flops 1 | bytes 1 | tf_op jit(solution)/shard_map/pallas_call | solution.py:44
  78.0 4.2 %collective-permute-done.19.refs_4_ = bf16[2,2,24,1536]{3,2,1,0:T(8,128)(2,1)S(1)} collective-permute-done((bf16[2,2,24,1536]{3,2,1,0:T(8,128)(2,1)S(1)}, bf16[2,2,24,1536]{3,2,1,0:T(8,128)(2,1)S(1)}, u32[]{:S(2)}, u32[]{:S(2)}) %collective-permute-start.19) | collective-permute-done | bytes 294944 | tf_op jit(solution)/shard_map/ppermute | solution.py:401
  86.2 2.3 shard_map.247
  93.1 12.6 %shard_map.248 = (bf16[1024,3072]{1,0:T(8,128)(2,1)}, f32[1024,3072]{1,0:T(8,128)}, bf16[8,192,768]{2,1,0:T(8,128)(2,1)}, bf16[8,192,768]{2,1,0:T(8,128)(2,1)}, f32[8,128]{1,0:T(8,128)S(1)}) custom-call(s32[4]{0:T(128)S(1)} %pad_add_fusion.refs_0_.refs_1_, bf16[1024,768]{1,0:T(8,128)(2,1)S(1)} %get-tuple-element.159.refs_1_.refs_2_, ...), custom_call_target="tpu_custom_call" | custom-call | flops 1 | bytes 1 | tf_op jit(solution)/shard_map/pallas_call | solution.py:44
  109.2 5.5 %shard_map.250 = (bf16[1024,3072]{1,0:T(8,128)(2,1)}, f32[1024,3072]{1,0:T(8,128)}, bf16[8,192,768]{2,1,0:T(8,128)(2,1)}, bf16[8,192,768]{2,1,0:T(8,128)(2,1)}, f32[8,128]{1,0:T(8,128)}) custom-call(s32[4]{0:T(128)S(1)} %pad_add_fusion.refs_0_.refs_1_, ...), custom_call_target="tpu_custom_call", output_to_operand_aliasing={{0}: (6, {}), {1}: (7, {}), {2}: (8, {}), {3}: (9, {})} | custom-call | flops 1 | bytes 1 | tf_op jit(solution)/shard_map/pallas_call | solution.py:44
  115.1 16.2 %shard_map.251 = (bf16[1024,3072]{1,0:T(8,128)(2,1)}, f32[1,3072]{1,0:T(1,128)S(1)}, bf16[8,48,3072]{2,1,0:T(8,128)(2,1)}, bf16[8,48,3072]{2,1,0:T(8,128)(2,1)}, f32[8,128]{1,0:T(8,128)S(1)}) custom-call(s32[4]{0:T(128)S(1)} %pad_add_fusion.refs_0_.refs_1_, bf16[1024,768]{1,0:T(8,128)(2,1)} %get-tuple-element.160.refs_2_.refs_1_, ...), custom_call_target="tpu_custom_call" | custom-call | flops 1 | bytes 1 | tf_op jit(solution)/shard_map/pallas_call | solution.py:44
  135.1 14.8 %shard_map.253 = (f32[1024,768]{1,0:T(8,128)}, bf16[1024,768]{1,0:T(8,128)(2,1)S(1)}, bf16[1024,768]{1,0:T(8,128)(2,1)S(1)}, f32[4,768]{1,0:T(4,128)S(1)}, f32[8,128]{1,0:T(8,128)S(1)}) custom-call(s32[4]{0:T(128)S(1)} %pad_add_fusion.refs_0_.refs_1_, bf16[1024,3072]{1,0:T(8,128)(2,1)} %get-tuple-element.181.refs_1_, bf16[8,48,3072]{2,1,0:T(8,128)(2,1)S(1)} %bitcast.27, ...), custom_call_target="tpu_custom_call" | custom-call | flops 1 | bytes 1 | tf_op jit(solution)/shard_map/pallas_call | solution.py:44
  152.9 13.0 %shard_map.255 = (bf16[1024,2304]{1,0:T(8,128)(2,1)S(1)}, f32[8,2304]{1,0:T(8,128)S(1)}, f32[8,128]{1,0:T(8,128)S(1)}) custom-call(s32[16]{0:T(128)S(1)} %reshape.65.refs_0_, bf16[1024,2304]{1,0:T(8,128)(2,1)} %get-tuple-element.179.refs_1_, bf16[1024,768]{1,0:T(8,128)(2,1)S(1)} %get-tuple-element.186.refs_2_, f32[96,128]{1,0:T(8,128)S(1)} %get-tuple-element.187.refs_3_, ...), custom_call_target="tpu_custom_call" | custom-call | flops 1 | bytes 1 | tf_op jit(solution)/shard_map/pallas_call | solution.py:44
  168.5 7.4 %shard_map.257 = (bf16[8,48,3072]{2,1,0:T(8,128)(2,1)S(1)}, bf16[8,48,3072]{2,1,0:T(8,128)(2,1)S(1)}, f32[8,128]{1,0:T(8,128)S(1)}) custom-call(s32[4]{0:T(128)S(1)} %pad_add_fusion.refs_0_.refs_1_, bf16[1024,768]{1,0:T(8,128)(2,1)S(1)} %copy-done.5, bf16[1024,768]{1,0:T(8,128)(2,1)S(1)} %get-tuple-element.153.refs_1_.refs_2_, ...), custom_call_target="tpu_custom_call" | custom-call | flops 1 | bytes 1 | tf_op jit(solution)/shard_map/pallas_call | solution.py:44
  177.7 11.1 %shard_map.258 = (bf16[1024,768]{1,0:T(8,128)(2,1)}, f32[1,768]{1,0:T(1,128)S(1)}, f32[8,128]{1,0:T(8,128)S(1)}) custom-call(s32[16]{0:T(128)S(1)} %reshape.65.refs_0_, s32[4]{0:T(128)S(1)} %pad_add_fusion.refs_0_.refs_1_, bf16[1024,3072]{1,0:T(8,128)(2,1)} %get-tuple-element.175.refs_2_, bf16[8,192,768]{2,1,0:T(8,128)(2,1)S(1)} %bitcast.32, ...), custom_call_target="tpu_custom_call" | custom-call | flops 1 | bytes 1 | tf_op jit(solution)/shard_map/pallas_call | solution.py:44
  196.8 12.4 %shard_map.261 = (f32[1024,768]{1,0:T(8,128)}, f32[2,768]{1,0:T(2,128)S(1)}, f32[8,128]{1,0:T(8,128)S(1)}) custom-call(s32[16]{0:T(128)S(1)} %reshape.65.refs_0_, s32[4]{0:T(128)S(1)} %pad_add_fusion.refs_0_.refs_1_, bf16[1024,2304]{1,0:T(8,128)(2,1)S(1)} %get-tuple-element.192.refs_3_.refs_2_, bf16[8,48,3072]{2,1,0:T(8,128)(2,1)S(1)} %bitcast.20, ...), custom_call_target="tpu_custom_call" | custom-call | flops 1 | bytes 1 | tf_op jit(solution)/shard_map/pallas_call | solution.py:44
  216.2 3.8 %collective-permute-done.40.refs_2_ = f32[14,768]{1,0:T(8,128)S(1)} collective-permute-done((f32[14,768]{1,0:T(8,128)S(1)}, f32[14,768]{1,0:T(8,128)S(1)}, u32[]{:S(2)}, u32[]{:S(2)}) %collective-permute-start.40) | collective-permute-done | bytes 43040 | tf_op jit(solution)/shard_map/ppermute | solution.py:401
  222.4 6.6 %collective-permute-start.42 = (bf16[24,3072]{1,0:T(8,128)(2,1)S(1)}, bf16[24,3072]{1,0:T(8,128)(2,1)S(1)}, u32[]{:S(2)}, u32[]{:S(2)}) collective-permute-start(bf16[24,3072]{1,0:T(8,128)(2,1)S(1)} %get-tuple-element.242), channel_id=1, source_target_pairs={{0,8},{1,9},{2,10},{3,11},{4,12},{5,13},{6,14},{7,15},{8,0},{9,1},... | collective-permute-start | bytes 442376 | tf_op jit(solution)/shard_map/ppermute | solution.py:401
  232.5 3.1 %collective-permute-done.45.refs_2_ = f32[14,768]{1,0:T(8,128)S(1)} collective-permute-done((f32[14,768]{1,0:T(8,128)S(1)}, f32[14,768]{1,0:T(8,128)S(1)}, u32[]{:S(2)}, u32[]{:S(2)}) %collective-permute-start.45) | collective-permute-done | bytes 43040 | tf_op jit(solution)/shard_map/ppermute | solution.py:401
  242.2 5.3 %collective-permute-done.47.refs_3_ = f32[14,768]{1,0:T(8,128)S(1)} collective-permute-done((f32[14,768]{1,0:T(8,128)S(1)}, f32[14,768]{1,0:T(8,128)S(1)}, u32[]{:S(2)}, u32[]{:S(2)}) %collective-permute-start.47) | collective-permute-done | bytes 43040 | tf_op jit(solution)/shard_map/ppermute | solution.py:401
  (181 shorter events, 86.1 us)
Async XLA Ops:
  7.8 14.0 %collective-permute-start.1 = (bf16[24,3072]{1,0:T(8,128)(2,1)S(1)}, bf16[24,3072]{1,0:T(8,128)(2,1)S(1)}, u32[]{:S(2)}, u32[]{:S(2)}) collective-permute-start(bf16[24,3072]{1,0:T(8,128)(2,1)S(1)} %get-tuple-element.138.refs_1_), channel_id=1, source_target_pairs={{0,16},{1,17},{2,18},{3,19},{4,20},{5,21},{6,22},{7,23},{8,24},{9,... | collective-permute-start | bytes 442376 | tf_op jit(solution)/shard_map/ppermute | solution.py:401
  52.2 16.6 %collective-permute-start.16 = (bf16[2,2,24,1536]{3,2,1,0:T(8,128)(2,1)S(1)}, bf16[2,2,24,1536]{3,2,1,0:T(8,128)(2,1)S(1)}, u32[]{:S(2)}, u32[]{:S(2)}) collective-permute-start(bf16[2,2,24,1536]{3,2,1,0:T(8,128)(2,1)S(1)} %get-tuple-element.149.refs_1_), channel_id=1, source_target_pairs={{0,16},{1,17},{2,18},{3,19},{4,20},{5,21},{6,22},{7,23},{8,24},{9,... | collective-permute-start | bytes 884744 | tf_op jit(solution)/shard_map/ppermute | solution.py:401
  52.4 16.4 %collective-permute-start.14 = (bf16[4,24,1536]{2,1,0:T(8,128)(2,1)S(1)}, bf16[4,24,1536]{2,1,0:T(8,128)(2,1)S(1)}, u32[]{:S(2)}, u32[]{:S(2)}) collective-permute-start(bf16[4,24,1536]{2,1,0:T(8,128)(2,1)S(1)} %get-tuple-element.155.refs_1_), channel_id=1, source_target_pairs={{0,4},{1,5},{2,6},{3,7},{4,0},{5,1},{6,2},{7,3},{8,12},{9,13},{10,... | collective-permute-start | bytes 884744 | tf_op jit(solution)/shard_map/ppermute | solution.py:401
  53.9 14.9 %collective-permute-start.15 = (bf16[4,24,1536]{2,1,0:T(8,128)(2,1)S(1)}, bf16[4,24,1536]{2,1,0:T(8,128)(2,1)S(1)}, u32[]{:S(2)}, u32[]{:S(2)}) collective-permute-start(bf16[4,24,1536]{2,1,0:T(8,128)(2,1)S(1)} %get-tuple-element.156.refs_3_), channel_id=1, source_target_pairs={{0,1},{1,0},{2,3},{3,2},{4,5},{5,4},{6,7},{7,6},{8,9},{9,8},{10,11... | collective-permute-start | bytes 884744 | tf_op jit(solution)/shard_map/ppermute | solution.py:401
  69.5 15.3 %collective-permute-start.17 = (bf16[2,4,24,1536]{3,2,1,0:T(8,128)(2,1)S(1)}, bf16[2,4,24,1536]{3,2,1,0:T(8,128)(2,1)S(1)}, u32[]{:S(2)}, u32[]{:S(2)}) collective-permute-start(bf16[2,4,24,1536]{3,2,1,0:T(8,128)(2,1)S(1)} %get-tuple-element.161.refs_1_), channel_id=1, source_target_pairs={{0,1},{1,0},{2,3},{3,2},{4,5},{5,4},{6,7},{7,6},{8,9},{9,8},{10,11... | collective-permute-start | bytes 1769480 | tf_op jit(solution)/shard_map/ppermute | solution.py:401
  70.4 15.0 %collective-permute-start.18 = (bf16[2,4,24,1536]{3,2,1,0:T(8,128)(2,1)S(1)}, bf16[2,4,24,1536]{3,2,1,0:T(8,128)(2,1)S(1)}, u32[]{:S(2)}, u32[]{:S(2)}) collective-permute-start(bf16[2,4,24,1536]{3,2,1,0:T(8,128)(2,1)S(1)} %get-tuple-element.162.refs_3_), channel_id=1, source_target_pairs={{0,4},{1,5},{2,6},{3,7},{4,0},{5,1},{6,2},{7,3},{8,12},{9,13},{10,... | collective-permute-start | bytes 1769480 | tf_op jit(solution)/shard_map/ppermute | solution.py:401
  88.6 17.1 %collective-permute-start.21 = (bf16[2,4,24,1536]{3,2,1,0:T(8,128)(2,1)S(1)}, bf16[2,4,24,1536]{3,2,1,0:T(8,128)(2,1)S(1)}, u32[]{:S(2)}, u32[]{:S(2)}) collective-permute-start(bf16[2,4,24,1536]{3,2,1,0:T(8,128)(2,1)S(1)} %get-tuple-element.171.refs_1_), channel_id=1, source_target_pairs={{0,1},{1,0},{2,3},{3,2},{4,5},{5,4},{6,7},{7,6},{8,9},{9,8},{10,11... | collective-permute-start | bytes 1769480 | tf_op jit(solution)/shard_map/ppermute | solution.py:401
  89.8 16.0 %collective-permute-start.22 = (bf16[2,4,24,1536]{3,2,1,0:T(8,128)(2,1)S(1)}, bf16[2,4,24,1536]{3,2,1,0:T(8,128)(2,1)S(1)}, u32[]{:S(2)}, u32[]{:S(2)}) collective-permute-start(bf16[2,4,24,1536]{3,2,1,0:T(8,128)(2,1)S(1)} %get-tuple-element.172.refs_3_), channel_id=1, source_target_pairs={{0,4},{1,5},{2,6},{3,7},{4,0},{5,1},{6,2},{7,3},{8,12},{9,13},{10,... | collective-permute-start | bytes 1769480 | tf_op jit(solution)/shard_map/ppermute | solution.py:401
  114.7 16.7 %collective-permute-start.24 = (bf16[8,192,768]{2,1,0:T(8,128)(2,1)}, bf16[8,192,768]{2,1,0:T(8,128)(2,1)S(1)}, u32[]{:S(2)}, u32[]{:S(2)}) collective-permute-start(bf16[8,192,768]{2,1,0:T(8,128)(2,1)} %get-tuple-element.183), channel_id=1, source_target_pairs={{0,2},{1,3},{2,0},{3,1},{4,6},{5,7},{6,4},{7,5},{8,10},{9,11},{10,... | collective-permute-start | bytes 7077896 | tf_op jit(solution)/shard_map/ppermute | solution.py:401
  131.3 18.6 %collective-permute-start.25 = (bf16[8,48,3072]{2,1,0:T(8,128)(2,1)}, bf16[8,48,3072]{2,1,0:T(8,128)(2,1)S(1)}, u32[]{:S(2)}, u32[]{:S(2)}) collective-permute-start(bf16[8,48,3072]{2,1,0:T(8,128)(2,1)} %get-tuple-element.189), channel_id=1, source_target_pairs={{0,2},{1,3},{2,0},{3,1},{4,6},{5,7},{6,4},{7,5},{8,10},{9,11},{10,... | collective-permute-start | bytes 7077896 | tf_op jit(solution)/shard_map/ppermute | solution.py:401
  132.7 33.2 %collective-permute-start.27 = (bf16[4,2,96,384]{3,2,1,0:T(8,128)(2,1)S(1)}, bf16[4,2,96,384]{3,2,1,0:T(8,128)(2,1)S(1)}, u32[]{:S(2)}, u32[]{:S(2)}) collective-permute-start(bf16[4,2,96,384]{3,2,1,0:T(8,128)(2,1)S(1)} %get-tuple-element.197), channel_id=1, source_target_pairs={{0,1},{1,0},{2,3},{3,2},{4,5},{5,4},{6,7},{7,6},{8,9},{9,8},{10,11... | collective-permute-start | bytes 1769480 | tf_op jit(solution)/shard_map/ppermute | solution.py:401
  133.9 32.0 %collective-permute-start.29 = (bf16[4,2,96,384]{3,2,1,0:T(8,128)(2,1)S(1)}, bf16[4,2,96,384]{3,2,1,0:T(8,128)(2,1)S(1)}, u32[]{:S(2)}, u32[]{:S(2)}) collective-permute-start(bf16[4,2,96,384]{3,2,1,0:T(8,128)(2,1)S(1)} %get-tuple-element.201), channel_id=1, source_target_pairs={{0,4},{1,5},{2,6},{3,7},{4,0},{5,1},{6,2},{7,3},{8,12},{9,13},{10,... | collective-permute-start | bytes 1769480 | tf_op jit(solution)/shard_map/ppermute | solution.py:401
  151.1 15.1 %collective-permute-start.26 = (bf16[4,2,24,1536]{3,2,1,0:T(8,128)(2,1)S(1)}, bf16[4,2,24,1536]{3,2,1,0:T(8,128)(2,1)S(1)}, u32[]{:S(2)}, u32[]{:S(2)}) collective-permute-start(bf16[4,2,24,1536]{3,2,1,0:T(8,128)(2,1)S(1)} %get-tuple-element.195), channel_id=1, source_target_pairs={{0,1},{1,0},{2,3},{3,2},{4,5},{5,4},{6,7},{7,6},{8,9},{9,8},{10,11... | collective-permute-start | bytes 1769480 | tf_op jit(solution)/shard_map/ppermute | solution.py:401
  152.3 14.7 %collective-permute-start.28 = (bf16[4,2,24,1536]{3,2,1,0:T(8,128)(2,1)S(1)}, bf16[4,2,24,1536]{3,2,1,0:T(8,128)(2,1)S(1)}, u32[]{:S(2)}, u32[]{:S(2)}) collective-permute-start(bf16[4,2,24,1536]{3,2,1,0:T(8,128)(2,1)S(1)} %get-tuple-element.199), channel_id=1, source_target_pairs={{0,4},{1,5},{2,6},{3,7},{4,0},{5,1},{6,2},{7,3},{8,12},{9,13},{10,... | collective-permute-start | bytes 1769480 | tf_op jit(solution)/shard_map/ppermute | solution.py:401
  176.0 16.5 %collective-permute-start.30 = (bf16[4,24,3072]{2,1,0:T(8,128)(2,1)S(1)}, bf16[4,24,3072]{2,1,0:T(8,128)(2,1)S(1)}, u32[]{:S(2)}, u32[]{:S(2)}) collective-permute-start(bf16[4,24,3072]{2,1,0:T(8,128)(2,1)S(1)} %get-tuple-element.208), channel_id=1, source_target_pairs={{0,4},{1,5},{2,6},{3,7},{4,0},{5,1},{6,2},{7,3},{8,12},{9,13},{10,... | collective-permute-start | bytes 1769480 | tf_op jit(solution)/shard_map/ppermute | solution.py:401
  176.6 15.9 %collective-permute-start.31 = (bf16[4,24,3072]{2,1,0:T(8,128)(2,1)S(1)}, bf16[4,24,3072]{2,1,0:T(8,128)(2,1)S(1)}, u32[]{:S(2)}, u32[]{:S(2)}) collective-permute-start(bf16[4,24,3072]{2,1,0:T(8,128)(2,1)S(1)} %get-tuple-element.210), channel_id=1, source_target_pairs={{0,1},{1,0},{2,3},{3,2},{4,5},{5,4},{6,7},{7,6},{8,9},{9,8},{10,11... | collective-permute-start | bytes 1769480 | tf_op jit(solution)/shard_map/ppermute | solution.py:401
  190.0 20.3 %collective-permute-start.33 = (bf16[4,2,24,1536]{3,2,1,0:T(8,128)(2,1)S(1)}, bf16[4,2,24,1536]{3,2,1,0:T(8,128)(2,1)S(1)}, u32[]{:S(2)}, u32[]{:S(2)}) collective-permute-start(bf16[4,2,24,1536]{3,2,1,0:T(8,128)(2,1)S(1)} %get-tuple-element.218), channel_id=1, source_target_pairs={{0,1},{1,0},{2,3},{3,2},{4,5},{5,4},{6,7},{7,6},{8,9},{9,8},{10,11... | collective-permute-start | bytes 1769480 | tf_op jit(solution)/shard_map/ppermute | solution.py:401
  191.0 19.4 %collective-permute-start.34 = (bf16[4,2,24,1536]{3,2,1,0:T(8,128)(2,1)S(1)}, bf16[4,2,24,1536]{3,2,1,0:T(8,128)(2,1)S(1)}, u32[]{:S(2)}, u32[]{:S(2)}) collective-permute-start(bf16[4,2,24,1536]{3,2,1,0:T(8,128)(2,1)S(1)} %get-tuple-element.220), channel_id=1, source_target_pairs={{0,4},{1,5},{2,6},{3,7},{4,0},{5,1},{6,2},{7,3},{8,12},{9,13},{10,... | collective-permute-start | bytes 1769480 | tf_op jit(solution)/shard_map/ppermute | solution.py:401
  193.3 16.0 %collective-permute-start.35 = (bf16[24,6144]{1,0:T(8,128)(2,1)S(1)}, bf16[24,6144]{1,0:T(8,128)(2,1)S(1)}, u32[]{:S(2)}, u32[]{:S(2)}) collective-permute-start(bf16[24,6144]{1,0:T(8,128)(2,1)S(1)} %get-tuple-element.222), channel_id=1, source_target_pairs={{0,8},{1,9},{2,10},{3,11},{4,12},{5,13},{6,14},{7,15},{8,0},{9,1},... | collective-permute-start | bytes 884744 | tf_op jit(solution)/shard_map/ppermute | solution.py:401
  194.0 16.3 %collective-permute-start.36 = (bf16[24,6144]{1,0:T(8,128)(2,1)S(1)}, bf16[24,6144]{1,0:T(8,128)(2,1)S(1)}, u32[]{:S(2)}, u32[]{:S(2)}) collective-permute-start(bf16[24,6144]{1,0:T(8,128)(2,1)S(1)} %get-tuple-element.223), channel_id=1, source_target_pairs={{0,24},{1,25},{2,26},{3,27},{4,28},{5,29},{6,30},{7,31},{8,16},{9,... | collective-permute-start | bytes 884744 | tf_op jit(solution)/shard_map/ppermute | solution.py:401
  196.0 25.7 %collective-permute-start.41 = (bf16[24,6144]{1,0:T(8,128)(2,1)S(1)}, bf16[24,6144]{1,0:T(8,128)(2,1)S(1)}, u32[]{:S(2)}, u32[]{:S(2)}) collective-permute-start(bf16[24,6144]{1,0:T(8,128)(2,1)S(1)} %get-tuple-element.240), channel_id=1, source_target_pairs={{0,16},{1,17},{2,18},{3,19},{4,20},{5,21},{6,22},{7,23},{8,24},{9,... | collective-permute-start | bytes 884744 | tf_op jit(solution)/shard_map/ppermute | solution.py:401
  222.4 16.1 %collective-permute-start.42 = (bf16[24,3072]{1,0:T(8,128)(2,1)S(1)}, bf16[24,3072]{1,0:T(8,128)(2,1)S(1)}, u32[]{:S(2)}, u32[]{:S(2)}) collective-permute-start(bf16[24,3072]{1,0:T(8,128)(2,1)S(1)} %get-tuple-element.242), channel_id=1, source_target_pairs={{0,8},{1,9},{2,10},{3,11},{4,12},{5,13},{6,14},{7,15},{8,0},{9,1},... | collective-permute-start | bytes 442376 | tf_op jit(solution)/shard_map/ppermute | solution.py:401
  229.0 18.6 %collective-permute-start.43 = (bf16[24,3072]{1,0:T(8,128)(2,1)S(1)}, bf16[24,3072]{1,0:T(8,128)(2,1)S(1)}, u32[]{:S(2)}, u32[]{:S(2)}) collective-permute-start(bf16[24,3072]{1,0:T(8,128)(2,1)S(1)} %get-tuple-element.243), channel_id=1, source_target_pairs={{0,16},{1,17},{2,18},{3,19},{4,20},{5,21},{6,22},{7,23},{8,24},{9,... | collective-permute-start | bytes 442376 | tf_op jit(solution)/shard_map/ppermute | solution.py:401
  229.4 18.2 %collective-permute-start.44 = (bf16[24,3072]{1,0:T(8,128)(2,1)S(1)}, bf16[24,3072]{1,0:T(8,128)(2,1)S(1)}, u32[]{:S(2)}, u32[]{:S(2)}) collective-permute-start(bf16[24,3072]{1,0:T(8,128)(2,1)S(1)} %get-tuple-element.244), channel_id=1, source_target_pairs={{0,24},{1,25},{2,26},{3,27},{4,28},{5,29},{6,30},{7,31},{8,16},{9,... | collective-permute-start | bytes 442376 | tf_op jit(solution)/shard_map/ppermute | solution.py:401
  (57 other events, 611.8 us)
where the time goes:
time: 250 us
  Pallas kernels  138 us (55%)
  starting transfers between devices  60.7 us (24%)
  waiting for transfers between devices  43.1 us (17%)
  local copies, waits for them, and re-layouts  6.35 us (3%)
    pallas_call x34, Pallas kernels, call(): pl.pallas_call(run, grid_spec=pltpu.PrefetchScalarGridSpec(num_scalar_pre...  138 us
    ppermute x49, starting transfers between devices, swap(): return lax.ppermute(v, AXES, [(i, i ^ mask) for i in range(32)])  60.7 us
    ppermute x49, waiting for transfers between devices, swap(): return lax.ppermute(v, AXES, [(i, i ^ mask) for i in range(32)])  43.1 us
    unnamed x65, local copies, waits for them, and re-layouts  6.22 us
  transfers between devices with their start and end apart: 49, of which 22 were waited for; matrix products, arithmetic and copies ran while one was open for 0% of the time, Pallas kernels for 47%

commit v1 on v0

--- a/solution.py
+++ b/solution.py
@@ -217,7 +217,7 @@
 
 def hidden_kernel(sc, n2, b2g, fc1_bias, own, other, act, slope, go, gs, scr):
     w1 = join(scr, sc[0], own, other)
-    for rows in pieces(n2.shape[0], 256):
+    for rows in pieces(n2.shape[0]):
         hidden = dot(n2[rows], w1) + fc1_bias[...]
         normal = 0.5 * (1.0 + lax.erf(hidden * 0.5**0.5))
         act[rows] = (hidden * normal).astype(BF16)
@@ -226,11 +226,7 @@
     part(sc[0], dot_tn(act[...], b2g[...]).astype(BF16), go, gs)
 
 
-def hidden_back_kernel(sc, b2g, n2, slope, own, other, hg, sums, go, gs, n2t, scr):
-    @pl.when(pl.program_id(0) == 0)
-    def _():
-        n2t[...] = n2[...].T
-
+def hidden_back_kernel(sc, b2g, n2, slope, own, other, hg, sums, go, gs, scr):
     w2 = join(scr, sc[0], own, other)
     total = jnp.zeros((8, sums.shape[1]), F32)
     for rows in pieces(b2g.shape[0], 256):
@@ -238,7 +234,7 @@
         hg[rows] = low
         total = total + eights(low.astype(F32))
     sums[...] = column_sum(total)
-    part(sc[0], dot(n2t[...], hg[...]).astype(BF16), go, gs)
+    part(sc[0], dot_tn(n2[...], hg[...]).astype(BF16), go, gs)
 
 
 def middle_back_kernel(sc, hg, own, other, po, ps, b1, x, up, gain, ls, mg, b1g, ag, sums, acc, scr, pscr, *, tiles):
@@ -343,27 +339,32 @@
 
 
 def input_back_kernel(grid_ref, sc, pg, own, other, x, mg, gain, out, sums, scr, acc, high, mid, *, images):
-    pack = pl.program_id(0)
-
-    @pl.when(pack == 0)
+    step = pl.program_id(0)
+    size, width = x.shape
+    per = out.shape[0] // size
+
+    @pl.when(step == 0)
     def _():
         join(scr, sc[0], own, other)
         sums[...] = jnp.zeros_like(sums)
 
-    width = x.shape[1]
     acc[...] = dot_nt(pg[...], scr[...].reshape(width, 3 * width))
     totals = [jnp.zeros((8, width), F32) for _ in range(2)]
-    for rows in pieces(acc.shape[0]):
+    for rows in pieces(size):
         grad = acc[rows]
         scaled, inverse = standardize(x[rows].astype(F32))
         back = mg[rows] + standardize_back(grad * gain[0:1], scaled, inverse)
         totals = [t + eights(v) for t, v in zip(totals, (grad * scaled, grad))]
         big = back.astype(BF16)
-        high[rows] = big
-        mid[rows] = (back - big.astype(F32)).astype(BF16)
+        at = pl.ds(pl.multiple_of(step % per * size + rows.start, 128), rows.size)
+        high[at] = big
+        mid[at] = (back - big.astype(F32)).astype(BF16)
     sums[...] += jnp.concatenate([column_sum(t) for t in totals], axis=0)
-    place = unplace(grid_ref, pack, images, x.shape[0])
-    out[...] = dot(place, high[...]) + dot(place, mid[...])
+
+    @pl.when(step % per == per - 1)
+    def _():
+        place = unplace(grid_ref, step // per, images, out.shape[0])
+        out[...] = dot(place, high[...]) + dot(place, mid[...])
 
 
 def layer_out_kernel(grid_ref, sc, act, own, other, x, b1, up, ls, fc2_bias, out, sums, acc, result, scr, *, images, tiles):
@@ -463,7 +464,7 @@
     shapes = [(rows, columns[0] + columns[1]), (rows, columns[2]), (rows, half), (rows, half)]
     scratch = [pltpu.VMEM(v.shape, F32) for v in arrays]
     outs = [(shape, BF16, full(shape)) for shape in shapes]
-    return call(kernel, (1,), (), [(v, full(v.shape)) for v in arrays], outs, scratch, (), mib=8)[:4]
+    return call(kernel, (1,), (), [(far(v), full(v.shape)) for v in arrays], outs, scratch, (), mib=8)[:4]
 
 
 def gather_pair(a, b, sc, after):
@@ -766,8 +767,8 @@
         [(far(b2g), whole), (far(n2), whole), (far(slope), hidden_tile), (fc2_own, fc2_blocks), (fc2_other, fc2_blocks)],
         [((rows, hidden), BF16, hidden_tile, "far"), ((1, hidden), F32, hidden_vec)]
         + [((COLUMNS, thin, hidden), BF16, column_blocks, "far")] * 2,
-        [turned_scr, fc2_scr],
-        mib=28,
+        [fc2_scr],
+        mib=26,
     )
     chain = []
     if swaps:
@@ -839,21 +840,22 @@
         token, fc_parts = fold_sends(fold_second(fc_parts, sc, [token]))
         chain = [token]
 
+    per = pack // tile
     input_grad, input_sums, token = call(
         partial(input_back_kernel, images=images),
-        (packs,),
+        (rows // tile,),
         (grid_flat, sc),
-        [(pg, pl.BlockSpec((pack, 3 * width), lambda i, *_: (i, 0))), (qp_own, qkv_blocks), (qp_other, qkv_blocks)]
-        + [(x, by_pack), (mg, by_pack), (norm_gain, vec2)],
-        [((rows, width), F32, by_pack, "far"), ((2, width), F32, vec2)],
-        [qkv_scr, pltpu.VMEM((pack, width), F32)] + [pltpu.VMEM((pack, width), BF16)] * 2,
+        [(pg, by_tile(3 * width)), (qp_own, qkv_blocks), (qp_other, qkv_blocks)]
+        + [(x, by_tile(width)), (mg, by_tile(width)), (norm_gain, vec2)],
+        [((rows, width), F32, pl.BlockSpec((pack, width), lambda i, *_: (i // per, 0)), "far"), ((2, width), F32, vec2)],
+        [qkv_scr, pltpu.VMEM((tile, width), F32)] + [pltpu.VMEM((pack, width), BF16)] * 2,
         chain,
-        mib=26,
+        mib=24,
     )
 
     chain = []
     if swaps:
-        qp_parts, token = fold_first(qp_parts, sc, [token, fc_parts[1], fc_parts[3]])
+        qp_parts, token = fold_first(qp_parts, sc, [token, fc_parts[1]])
         chain = [token]
 
     def gather_sums(input_sums, middle, proj, fc2, out, fc1, to):
@@ -883,7 +885,7 @@
             fc_runs += [(1, k * fc2_rows_of + half * n2_runs + i, width // 128) for k in range(tiles) for i in range(n2_runs)]
         sums, token = reduce_level(reduce_sends(sums, (CORE,)), (0,), sc, [token])
         sums, token = reduce_level(reduce_sends(sums, (Y,)), (2,), sc, [token])
-        token, qp_parts = fold_sends(fold_second(qp_parts, sc, [token, fc_parts[2]]))
+        token, qp_parts = fold_sends(fold_second(qp_parts, sc, [token, fc_parts[2], fc_parts[3]]))
         sums, token = reduce_level(reduce_sends(sums, (X,)), (1,), sc, [token])
         fc1_grad, fc2_grad, token = fold_last(fc_parts, (fc1_rows.shape, fc2_rows.shape), fc_runs, [token, qp_parts[1]])
         line = lambda i: pl.ds(i * width, width)

time: 250 us -> 241 us (0.964)
  local copies, waits for them, and re-layouts: 6.35 us -> 2.55 us
    unnamed x65 -> x57, local copies, waits for them, and re-layouts: 6.22 us -> 2.43 us
  transfers between devices with their start and end apart: 49 -> 49, of which waited for: 22 -> 21; matrix products, arithmetic and copies ran while one was open for 0% -> 0% of each run, Pallas kernels for 47% -> 47%
where the time goes in v1:
time: 241 us
  Pallas kernels  137 us (57%)
  starting transfers between devices  58.8 us (24%)
  waiting for transfers between devices  40.9 us (17%)
  local copies, waits for them, and re-layouts  2.55 us (1%)
    pallas_call x34, Pallas kernels, call(): pl.pallas_call(run, grid_spec=pltpu.PrefetchScalarGridSpec(num_scalar_pre...  137 us
    ppermute x49, starting transfers between devices, swap(): return lax.ppermute(v, AXES, [(i, i ^ mask) for i in range(32)])  58.8 us
    ppermute x49, waiting for transfers between devices, swap(): return lax.ppermute(v, AXES, [(i, i ^ mask) for i in range(32)])  40.9 us
  transfers between devices with their start and end apart: 49, of which 21 were waited for; matrix products, arithmetic and copies ran while one was open for 0% of the time, Pallas kernels for 47%

profile of v1, /device:TPU:0, one launch (start us, length us, event | category | flops | bytes accessed | tf_op | source)
XLA Modules:
  0.0 240.7 jit_solution(3679718211521354662)
XLA Ops:
  2.4 3.0 %collective-permute-start = (bf16[24,3072]{1,0:T(8,128)(2,1)S(1)}, bf16[24,3072]{1,0:T(8,128)(2,1)S(1)}, u32[]{:S(2)}, u32[]{:S(2)}) collective-permute-start(bf16[24,3072]{1,0:T(8,128)(2,1)S(1)} %get-tuple-element.138.refs_1_), channel_id=1, source_target_pairs={{0,8},{1,9},{2,10},{3,11},{4,12},{5,13},{6,14},{7,15},{8,0},{9,1},... | collective-permute-start | bytes 442376 | tf_op jit(solution)/shard_map/ppermute | solution.py:402
  5.4 2.6 %collective-permute-start.1 = (bf16[24,3072]{1,0:T(8,128)(2,1)S(1)}, bf16[24,3072]{1,0:T(8,128)(2,1)S(1)}, u32[]{:S(2)}, u32[]{:S(2)}) collective-permute-start(bf16[24,3072]{1,0:T(8,128)(2,1)S(1)} %get-tuple-element.138.refs_1_), channel_id=1, source_target_pairs={{0,16},{1,17},{2,18},{3,19},{4,20},{5,21},{6,22},{7,23},{8,24},{9,... | collective-permute-start | bytes 442376 | tf_op jit(solution)/shard_map/ppermute | solution.py:402
  14.0 5.3 %collective-permute-done.1.refs_3_ = bf16[24,3072]{1,0:T(8,128)(2,1)S(1)} collective-permute-done((bf16[24,3072]{1,0:T(8,128)(2,1)S(1)}, bf16[24,3072]{1,0:T(8,128)(2,1)S(1)}, u32[]{:S(2)}, u32[]{:S(2)}) %collective-permute-start.1) | collective-permute-done | bytes 147488 | tf_op jit(solution)/shard_map/ppermute | solution.py:402
  25.9 2.5 %collective-permute-start.8 = (bf16[24,3072]{1,0:T(8,128)(2,1)S(1)}, bf16[24,3072]{1,0:T(8,128)(2,1)S(1)}, u32[]{:S(2)}, u32[]{:S(2)}) collective-permute-start(bf16[24,3072]{1,0:T(8,128)(2,1)S(1)} %get-tuple-element.143.refs_1_), channel_id=1, source_target_pairs={{0,24},{1,25},{2,26},{3,27},{4,28},{5,29},{6,30},{7,31},{8,16},{9,... | collective-permute-start | bytes 442376 | tf_op jit(solution)/shard_map/ppermute | solution.py:402
  30.3 3.2 %collective-permute-done.8.refs_6_.refs_4_ = bf16[24,3072]{1,0:T(8,128)(2,1)S(1)} collective-permute-done((bf16[24,3072]{1,0:T(8,128)(2,1)S(1)}, bf16[24,3072]{1,0:T(8,128)(2,1)S(1)}, u32[]{:S(2)}, u32[]{:S(2)}) %collective-permute-start.8) | collective-permute-done | bytes 147488 | tf_op jit(solution)/shard_map/ppermute | solution.py:402
  35.3 2.6 %collective-permute-start.11 = (bf16[24,3072]{1,0:T(8,128)(2,1)S(1)}, bf16[24,3072]{1,0:T(8,128)(2,1)S(1)}, u32[]{:S(2)}, u32[]{:S(2)}) collective-permute-start(bf16[24,3072]{1,0:T(8,128)(2,1)S(1)} %get-tuple-element.143.refs_1_), channel_id=1, source_target_pairs={{0,16},{1,17},{2,18},{3,19},{4,20},{5,21},{6,22},{7,23},{8,24},{9,... | collective-permute-start | bytes 442376 | tf_op jit(solution)/shard_map/ppermute | solution.py:402
  38.2 7.7 %shard_map.240 = (bf16[1024,768]{1,0:T(8,128)(2,1)}, bf16[1024,768]{1,0:T(8,128)(2,1)}, bf16[1024,768]{1,0:T(8,128)(2,1)}, bf16[1024,768]{1,0:T(8,128)(2,1)}, f3...) custom-call(s32[16]{0:T(128)S(1)} %reshape.65.refs_0_, bf16[1024,768]{1,0:T(8,128)(2,1)} %refs_1_.3, bf16[1024,768]{1,0:T(8,128)(2,1)} %refs_2_.3, ...), custom_call_target="tpu_custom_call" | custom-call | flops 1 | bytes 1 | tf_op jit(solution)/shard_map/pallas_call | solution.py:44
  47.5 2.3 shard_map.242
  54.4 10.5 %shard_map.243 = (bf16[1024,2304]{1,0:T(8,128)(2,1)}, bf16[1024,768]{1,0:T(8,128)(2,1)S(1)}, f32[96,128]{1,0:T(8,128)S(1)}, f32[8,128]{1,0:T(8,128)S(1)}) custom-call(s32[16]{0:T(128)S(1)} %reshape.65.refs_0_, s32[4]{0:T(128)S(1)} %pad_add_fusion.refs_0_.refs_1_, bf16[1024,768]{1,0:T(8,128)(2,1)} %get-tuple-element.145.refs_2_.refs_1_, ...), custom_call_target="tpu_custom_call" | custom-call | flops 1 | bytes 1 | tf_op jit(solution)/shard_map/pallas_call | solution.py:44
  71.3 4.3 %shard_map.245 = (f32[1024,768]{1,0:T(8,128)}, bf16[1024,768]{1,0:T(8,128)(2,1)S(1)}, f32[8,128]{1,0:T(8,128)S(1)}) custom-call(s32[4]{0:T(128)S(1)} %pad_add_fusion.refs_0_.refs_1_, bf16[1024,768]{1,0:T(8,128)(2,1)S(1)} %get-tuple-element.153.refs_1_.refs_2_, bf16[1024,768]{1,0:T(8,128)(2,1)S(1)} %copy-done, f32[2,768]{1,0:T(2,128)S(1)} %copy-done.16, ...), custom_call_target="tpu_custom_call" | custom-call | flops 1 | bytes 1 | tf_op jit(solution)/shard_map/pallas_call | solution.py:44
  75.6 4.2 %collective-permute-done.19.refs_4_ = bf16[2,2,24,1536]{3,2,1,0:T(8,128)(2,1)S(1)} collective-permute-done((bf16[2,2,24,1536]{3,2,1,0:T(8,128)(2,1)S(1)}, bf16[2,2,24,1536]{3,2,1,0:T(8,128)(2,1)S(1)}, u32[]{:S(2)}, u32[]{:S(2)}) %collective-permute-start.19) | collective-permute-done | bytes 294944 | tf_op jit(solution)/shard_map/ppermute | solution.py:402
  83.8 2.3 shard_map.247
  90.8 12.0 %shard_map.248 = (bf16[1024,3072]{1,0:T(8,128)(2,1)}, f32[1024,3072]{1,0:T(8,128)}, bf16[8,192,768]{2,1,0:T(8,128)(2,1)}, bf16[8,192,768]{2,1,0:T(8,128)(2,1)}, f32[8,128]{1,0:T(8,128)S(1)}) custom-call(s32[4]{0:T(128)S(1)} %pad_add_fusion.refs_0_.refs_1_, bf16[1024,768]{1,0:T(8,128)(2,1)S(1)} %get-tuple-element.159.refs_1_.refs_2_, ...), custom_call_target="tpu_custom_call" | custom-call | flops 1 | bytes 1 | tf_op jit(solution)/shard_map/pallas_call | solution.py:44
  106.3 5.2 %shard_map.250 = (bf16[1024,3072]{1,0:T(8,128)(2,1)}, f32[1024,3072]{1,0:T(8,128)}, bf16[8,192,768]{2,1,0:T(8,128)(2,1)}, bf16[8,192,768]{2,1,0:T(8,128)(2,1)}, f32[8,128]{1,0:T(8,128)}) custom-call(s32[4]{0:T(128)S(1)} %pad_add_fusion.refs_0_.refs_1_, ...), custom_call_target="tpu_custom_call", output_to_operand_aliasing={{0}: (6, {}), {1}: (7, {}), {2}: (8, {}), {3}: (9, {})} | custom-call | flops 1 | bytes 1 | tf_op jit(solution)/shard_map/pallas_call | solution.py:44
  111.9 15.6 %shard_map.251 = (bf16[1024,3072]{1,0:T(8,128)(2,1)}, f32[1,3072]{1,0:T(1,128)S(1)}, bf16[8,48,3072]{2,1,0:T(8,128)(2,1)}, bf16[8,48,3072]{2,1,0:T(8,128)(2,1)}, f32[8,128]{1,0:T(8,128)S(1)}) custom-call(s32[4]{0:T(128)S(1)} %pad_add_fusion.refs_0_.refs_1_, bf16[1024,768]{1,0:T(8,128)(2,1)} %get-tuple-element.160.refs_2_.refs_1_, ...), custom_call_target="tpu_custom_call" | custom-call | flops 1 | bytes 1 | tf_op jit(solution)/shard_map/pallas_call | solution.py:44
  132.2 14.8 %shard_map.253 = (f32[1024,768]{1,0:T(8,128)}, bf16[1024,768]{1,0:T(8,128)(2,1)S(1)}, bf16[1024,768]{1,0:T(8,128)(2,1)S(1)}, f32[4,768]{1,0:T(4,128)S(1)}, f32[8,128]{1,0:T(8,128)S(1)}) custom-call(s32[4]{0:T(128)S(1)} %pad_add_fusion.refs_0_.refs_1_, bf16[1024,3072]{1,0:T(8,128)(2,1)} %get-tuple-element.181.refs_1_, bf16[8,48,3072]{2,1,0:T(8,128)(2,1)S(1)} %bitcast.27, ...), custom_call_target="tpu_custom_call" | custom-call | flops 1 | bytes 1 | tf_op jit(solution)/shard_map/pallas_call | solution.py:44
  150.0 12.8 %shard_map.255 = (bf16[1024,2304]{1,0:T(8,128)(2,1)S(1)}, f32[8,2304]{1,0:T(8,128)S(1)}, f32[8,128]{1,0:T(8,128)S(1)}) custom-call(s32[16]{0:T(128)S(1)} %reshape.65.refs_0_, bf16[1024,2304]{1,0:T(8,128)(2,1)} %get-tuple-element.179.refs_1_, bf16[1024,768]{1,0:T(8,128)(2,1)S(1)} %get-tuple-element.186.refs_2_, f32[96,128]{1,0:T(8,128)S(1)} %get-tuple-element.187.refs_3_, ...), custom_call_target="tpu_custom_call" | custom-call | flops 1 | bytes 1 | tf_op jit(solution)/shard_map/pallas_call | solution.py:44
  166.0 7.6 %shard_map.257 = (bf16[8,48,3072]{2,1,0:T(8,128)(2,1)S(1)}, bf16[8,48,3072]{2,1,0:T(8,128)(2,1)S(1)}, f32[8,128]{1,0:T(8,128)S(1)}) custom-call(s32[4]{0:T(128)S(1)} %pad_add_fusion.refs_0_.refs_1_, bf16[1024,768]{1,0:T(8,128)(2,1)S(1)} %copy-done.5, bf16[1024,768]{1,0:T(8,128)(2,1)S(1)} %get-tuple-element.153.refs_1_.refs_2_, ...), custom_call_target="tpu_custom_call" | custom-call | flops 1 | bytes 1 | tf_op jit(solution)/shard_map/pallas_call | solution.py:44
  175.5 11.1 %shard_map.258 = (bf16[1024,768]{1,0:T(8,128)(2,1)}, f32[1,768]{1,0:T(1,128)S(1)}, f32[8,128]{1,0:T(8,128)S(1)}) custom-call(s32[16]{0:T(128)S(1)} %reshape.65.refs_0_, s32[4]{0:T(128)S(1)} %pad_add_fusion.refs_0_.refs_1_, bf16[1024,3072]{1,0:T(8,128)(2,1)} %get-tuple-element.175.refs_2_, bf16[8,192,768]{2,1,0:T(8,128)(2,1)S(1)} %bitcast.32, ...), custom_call_target="tpu_custom_call" | custom-call | flops 1 | bytes 1 | tf_op jit(solution)/shard_map/pallas_call | solution.py:44
  195.4 10.2 %shard_map.261 = (f32[1024,768]{1,0:T(8,128)}, f32[2,768]{1,0:T(2,128)S(1)}, f32[8,128]{1,0:T(8,128)S(1)}) custom-call(s32[16]{0:T(128)S(1)} %reshape.65.refs_0_, s32[4]{0:T(128)S(1)} %pad_add_fusion.refs_0_.refs_1_, bf16[1024,2304]{1,0:T(8,128)(2,1)S(1)} %get-tuple-element.192.refs_3_.refs_2_, bf16[8,48,3072]{2,1,0:T(8,128)(2,1)S(1)} %bitcast.20, ...), custom_call_target="tpu_custom_call" | custom-call | flops 1 | bytes 1 | tf_op jit(solution)/shard_map/pallas_call | solution.py:44
  211.6 4.2 %collective-permute-done.39.refs_2_ = f32[14,768]{1,0:T(8,128)S(1)} collective-permute-done((f32[14,768]{1,0:T(8,128)S(1)}, f32[14,768]{1,0:T(8,128)S(1)}, u32[]{:S(2)}, u32[]{:S(2)}) %collective-permute-start.39) | collective-permute-done | bytes 43040 | tf_op jit(solution)/shard_map/ppermute | solution.py:402
  217.1 3.9 %collective-permute-start.42 = (bf16[24,3072]{1,0:T(8,128)(2,1)S(1)}, bf16[24,3072]{1,0:T(8,128)(2,1)S(1)}, u32[]{:S(2)}, u32[]{:S(2)}) collective-permute-start(bf16[24,3072]{1,0:T(8,128)(2,1)S(1)} %get-tuple-element.242), channel_id=1, source_target_pairs={{0,8},{1,9},{2,10},{3,11},{4,12},{5,13},{6,14},{7,15},{8,0},{9,1},... | collective-permute-start | bytes 442376 | tf_op jit(solution)/shard_map/ppermute | solution.py:402
  224.4 3.1 %collective-permute-done.45.refs_2_ = f32[14,768]{1,0:T(8,128)S(1)} collective-permute-done((f32[14,768]{1,0:T(8,128)S(1)}, f32[14,768]{1,0:T(8,128)S(1)}, u32[]{:S(2)}, u32[]{:S(2)}) %collective-permute-start.45) | collective-permute-done | bytes 43040 | tf_op jit(solution)/shard_map/ppermute | solution.py:402
  233.8 4.9 %collective-permute-done.47.refs_3_ = f32[14,768]{1,0:T(8,128)S(1)} collective-permute-done((f32[14,768]{1,0:T(8,128)S(1)}, f32[14,768]{1,0:T(8,128)S(1)}, u32[]{:S(2)}, u32[]{:S(2)}) %collective-permute-start.47) | collective-permute-done | bytes 43040 | tf_op jit(solution)/shard_map/ppermute | solution.py:402
  (173 shorter events, 83.6 us)
Async XLA Ops:
  5.4 14.0 %collective-permute-start.1 = (bf16[24,3072]{1,0:T(8,128)(2,1)S(1)}, bf16[24,3072]{1,0:T(8,128)(2,1)S(1)}, u32[]{:S(2)}, u32[]{:S(2)}) collective-permute-start(bf16[24,3072]{1,0:T(8,128)(2,1)S(1)} %get-tuple-element.138.refs_1_), channel_id=1, source_target_pairs={{0,16},{1,17},{2,18},{3,19},{4,20},{5,21},{6,22},{7,23},{8,24},{9,... | collective-permute-start | bytes 442376 | tf_op jit(solution)/shard_map/ppermute | solution.py:402
  49.8 16.6 %collective-permute-start.16 = (bf16[2,2,24,1536]{3,2,1,0:T(8,128)(2,1)S(1)}, bf16[2,2,24,1536]{3,2,1,0:T(8,128)(2,1)S(1)}, u32[]{:S(2)}, u32[]{:S(2)}) collective-permute-start(bf16[2,2,24,1536]{3,2,1,0:T(8,128)(2,1)S(1)} %get-tuple-element.149.refs_1_), channel_id=1, source_target_pairs={{0,16},{1,17},{2,18},{3,19},{4,20},{5,21},{6,22},{7,23},{8,24},{9,... | collective-permute-start | bytes 884744 | tf_op jit(solution)/shard_map/ppermute | solution.py:402
  50.0 16.4 %collective-permute-start.14 = (bf16[4,24,1536]{2,1,0:T(8,128)(2,1)S(1)}, bf16[4,24,1536]{2,1,0:T(8,128)(2,1)S(1)}, u32[]{:S(2)}, u32[]{:S(2)}) collective-permute-start(bf16[4,24,1536]{2,1,0:T(8,128)(2,1)S(1)} %get-tuple-element.155.refs_1_), channel_id=1, source_target_pairs={{0,4},{1,5},{2,6},{3,7},{4,0},{5,1},{6,2},{7,3},{8,12},{9,13},{10,... | collective-permute-start | bytes 884744 | tf_op jit(solution)/shard_map/ppermute | solution.py:402
  51.5 14.9 %collective-permute-start.15 = (bf16[4,24,1536]{2,1,0:T(8,128)(2,1)S(1)}, bf16[4,24,1536]{2,1,0:T(8,128)(2,1)S(1)}, u32[]{:S(2)}, u32[]{:S(2)}) collective-permute-start(bf16[4,24,1536]{2,1,0:T(8,128)(2,1)S(1)} %get-tuple-element.156.refs_3_), channel_id=1, source_target_pairs={{0,1},{1,0},{2,3},{3,2},{4,5},{5,4},{6,7},{7,6},{8,9},{9,8},{10,11... | collective-permute-start | bytes 884744 | tf_op jit(solution)/shard_map/ppermute | solution.py:402
  67.1 15.3 %collective-permute-start.17 = (bf16[2,4,24,1536]{3,2,1,0:T(8,128)(2,1)S(1)}, bf16[2,4,24,1536]{3,2,1,0:T(8,128)(2,1)S(1)}, u32[]{:S(2)}, u32[]{:S(2)}) collective-permute-start(bf16[2,4,24,1536]{3,2,1,0:T(8,128)(2,1)S(1)} %get-tuple-element.161.refs_1_), channel_id=1, source_target_pairs={{0,1},{1,0},{2,3},{3,2},{4,5},{5,4},{6,7},{7,6},{8,9},{9,8},{10,11... | collective-permute-start | bytes 1769480 | tf_op jit(solution)/shard_map/ppermute | solution.py:402
  68.0 15.0 %collective-permute-start.18 = (bf16[2,4,24,1536]{3,2,1,0:T(8,128)(2,1)S(1)}, bf16[2,4,24,1536]{3,2,1,0:T(8,128)(2,1)S(1)}, u32[]{:S(2)}, u32[]{:S(2)}) collective-permute-start(bf16[2,4,24,1536]{3,2,1,0:T(8,128)(2,1)S(1)} %get-tuple-element.162.refs_3_), channel_id=1, source_target_pairs={{0,4},{1,5},{2,6},{3,7},{4,0},{5,1},{6,2},{7,3},{8,12},{9,13},{10,... | collective-permute-start | bytes 1769480 | tf_op jit(solution)/shard_map/ppermute | solution.py:402
  86.2 16.5 %collective-permute-start.21 = (bf16[2,4,24,1536]{3,2,1,0:T(8,128)(2,1)S(1)}, bf16[2,4,24,1536]{3,2,1,0:T(8,128)(2,1)S(1)}, u32[]{:S(2)}, u32[]{:S(2)}) collective-permute-start(bf16[2,4,24,1536]{3,2,1,0:T(8,128)(2,1)S(1)} %get-tuple-element.171.refs_1_), channel_id=1, source_target_pairs={{0,1},{1,0},{2,3},{3,2},{4,5},{5,4},{6,7},{7,6},{8,9},{9,8},{10,11... | collective-permute-start | bytes 1769480 | tf_op jit(solution)/shard_map/ppermute | solution.py:402
  87.4 15.4 %collective-permute-start.22 = (bf16[2,4,24,1536]{3,2,1,0:T(8,128)(2,1)S(1)}, bf16[2,4,24,1536]{3,2,1,0:T(8,128)(2,1)S(1)}, u32[]{:S(2)}, u32[]{:S(2)}) collective-permute-start(bf16[2,4,24,1536]{3,2,1,0:T(8,128)(2,1)S(1)} %get-tuple-element.172.refs_3_), channel_id=1, source_target_pairs={{0,4},{1,5},{2,6},{3,7},{4,0},{5,1},{6,2},{7,3},{8,12},{9,13},{10,... | collective-permute-start | bytes 1769480 | tf_op jit(solution)/shard_map/ppermute | solution.py:402
  111.5 16.2 %collective-permute-start.24 = (bf16[8,192,768]{2,1,0:T(8,128)(2,1)}, bf16[8,192,768]{2,1,0:T(8,128)(2,1)S(1)}, u32[]{:S(2)}, u32[]{:S(2)}) collective-permute-start(bf16[8,192,768]{2,1,0:T(8,128)(2,1)} %get-tuple-element.183), channel_id=1, source_target_pairs={{0,2},{1,3},{2,0},{3,1},{4,6},{5,7},{6,4},{7,5},{8,10},{9,11},{10,... | collective-permute-start | bytes 7077896 | tf_op jit(solution)/shard_map/ppermute | solution.py:402
  127.5 19.5 %collective-permute-start.25 = (bf16[8,48,3072]{2,1,0:T(8,128)(2,1)}, bf16[8,48,3072]{2,1,0:T(8,128)(2,1)S(1)}, u32[]{:S(2)}, u32[]{:S(2)}) collective-permute-start(bf16[8,48,3072]{2,1,0:T(8,128)(2,1)} %get-tuple-element.189), channel_id=1, source_target_pairs={{0,2},{1,3},{2,0},{3,1},{4,6},{5,7},{6,4},{7,5},{8,10},{9,11},{10,... | collective-permute-start | bytes 7077896 | tf_op jit(solution)/shard_map/ppermute | solution.py:402
  129.9 32.9 %collective-permute-start.27 = (bf16[4,2,96,384]{3,2,1,0:T(8,128)(2,1)}, bf16[4,2,96,384]{3,2,1,0:T(8,128)(2,1)S(1)}, u32[]{:S(2)}, u32[]{:S(2)}) collective-permute-start(bf16[4,2,96,384]{3,2,1,0:T(8,128)(2,1)} %get-tuple-element.197), channel_id=1, source_target_pairs={{0,1},{1,0},{2,3},{3,2},{4,5},{5,4},{6,7},{7,6},{8,9},{9,8},{10,11... | collective-permute-start | bytes 1769480 | tf_op jit(solution)/shard_map/ppermute | solution.py:402
  131.0 31.8 %collective-permute-start.29 = (bf16[4,2,96,384]{3,2,1,0:T(8,128)(2,1)S(1)}, bf16[4,2,96,384]{3,2,1,0:T(8,128)(2,1)S(1)}, u32[]{:S(2)}, u32[]{:S(2)}) collective-permute-start(bf16[4,2,96,384]{3,2,1,0:T(8,128)(2,1)S(1)} %get-tuple-element.201), channel_id=1, source_target_pairs={{0,4},{1,5},{2,6},{3,7},{4,0},{5,1},{6,2},{7,3},{8,12},{9,13},{10,... | collective-permute-start | bytes 1769480 | tf_op jit(solution)/shard_map/ppermute | solution.py:402
  148.2 15.1 %collective-permute-start.26 = (bf16[4,2,24,1536]{3,2,1,0:T(8,128)(2,1)S(1)}, bf16[4,2,24,1536]{3,2,1,0:T(8,128)(2,1)S(1)}, u32[]{:S(2)}, u32[]{:S(2)}) collective-permute-start(bf16[4,2,24,1536]{3,2,1,0:T(8,128)(2,1)S(1)} %get-tuple-element.195), channel_id=1, source_target_pairs={{0,1},{1,0},{2,3},{3,2},{4,5},{5,4},{6,7},{7,6},{8,9},{9,8},{10,11... | collective-permute-start | bytes 1769480 | tf_op jit(solution)/shard_map/ppermute | solution.py:402
  149.5 14.7 %collective-permute-start.28 = (bf16[4,2,24,1536]{3,2,1,0:T(8,128)(2,1)S(1)}, bf16[4,2,24,1536]{3,2,1,0:T(8,128)(2,1)S(1)}, u32[]{:S(2)}, u32[]{:S(2)}) collective-permute-start(bf16[4,2,24,1536]{3,2,1,0:T(8,128)(2,1)S(1)} %get-tuple-element.199), channel_id=1, source_target_pairs={{0,4},{1,5},{2,6},{3,7},{4,0},{5,1},{6,2},{7,3},{8,12},{9,13},{10,... | collective-permute-start | bytes 1769480 | tf_op jit(solution)/shard_map/ppermute | solution.py:402
  173.7 16.4 %collective-permute-start.30 = (bf16[4,24,3072]{2,1,0:T(8,128)(2,1)}, bf16[4,24,3072]{2,1,0:T(8,128)(2,1)S(1)}, u32[]{:S(2)}, u32[]{:S(2)}) collective-permute-start(bf16[4,24,3072]{2,1,0:T(8,128)(2,1)} %get-tuple-element.208), channel_id=1, source_target_pairs={{0,4},{1,5},{2,6},{3,7},{4,0},{5,1},{6,2},{7,3},{8,12},{9,13},{10,... | collective-permute-start | bytes 1769480 | tf_op jit(solution)/shard_map/ppermute | solution.py:402
  174.4 15.8 %collective-permute-start.31 = (bf16[4,24,3072]{2,1,0:T(8,128)(2,1)S(1)}, bf16[4,24,3072]{2,1,0:T(8,128)(2,1)S(1)}, u32[]{:S(2)}, u32[]{:S(2)}) collective-permute-start(bf16[4,24,3072]{2,1,0:T(8,128)(2,1)S(1)} %get-tuple-element.210), channel_id=1, source_target_pairs={{0,1},{1,0},{2,3},{3,2},{4,5},{5,4},{6,7},{7,6},{8,9},{9,8},{10,11... | collective-permute-start | bytes 1769480 | tf_op jit(solution)/shard_map/ppermute | solution.py:402
  187.7 17.9 %collective-permute-start.33 = (bf16[4,2,24,1536]{3,2,1,0:T(8,128)(2,1)S(1)}, bf16[4,2,24,1536]{3,2,1,0:T(8,128)(2,1)S(1)}, u32[]{:S(2)}, u32[]{:S(2)}) collective-permute-start(bf16[4,2,24,1536]{3,2,1,0:T(8,128)(2,1)S(1)} %get-tuple-element.218), channel_id=1, source_target_pairs={{0,1},{1,0},{2,3},{3,2},{4,5},{5,4},{6,7},{7,6},{8,9},{9,8},{10,11... | collective-permute-start | bytes 1769480 | tf_op jit(solution)/shard_map/ppermute | solution.py:402
  188.7 16.9 %collective-permute-start.34 = (bf16[4,2,24,1536]{3,2,1,0:T(8,128)(2,1)S(1)}, bf16[4,2,24,1536]{3,2,1,0:T(8,128)(2,1)S(1)}, u32[]{:S(2)}, u32[]{:S(2)}) collective-permute-start(bf16[4,2,24,1536]{3,2,1,0:T(8,128)(2,1)S(1)} %get-tuple-element.220), channel_id=1, source_target_pairs={{0,4},{1,5},{2,6},{3,7},{4,0},{5,1},{6,2},{7,3},{8,12},{9,13},{10,... | collective-permute-start | bytes 1769480 | tf_op jit(solution)/shard_map/ppermute | solution.py:402
  191.0 14.6 %collective-permute-start.35 = (bf16[24,6144]{1,0:T(8,128)(2,1)S(1)}, bf16[24,6144]{1,0:T(8,128)(2,1)S(1)}, u32[]{:S(2)}, u32[]{:S(2)}) collective-permute-start(bf16[24,6144]{1,0:T(8,128)(2,1)S(1)} %get-tuple-element.222), channel_id=1, source_target_pairs={{0,8},{1,9},{2,10},{3,11},{4,12},{5,13},{6,14},{7,15},{8,0},{9,1},... | collective-permute-start | bytes 884744 | tf_op jit(solution)/shard_map/ppermute | solution.py:402
  191.8 24.6 %collective-permute-start.40 = (bf16[24,6144]{1,0:T(8,128)(2,1)S(1)}, bf16[24,6144]{1,0:T(8,128)(2,1)S(1)}, u32[]{:S(2)}, u32[]{:S(2)}) collective-permute-start(bf16[24,6144]{1,0:T(8,128)(2,1)S(1)} %get-tuple-element.239), channel_id=1, source_target_pairs={{0,16},{1,17},{2,18},{3,19},{4,20},{5,21},{6,22},{7,23},{8,24},{9,... | collective-permute-start | bytes 884744 | tf_op jit(solution)/shard_map/ppermute | solution.py:402
  193.4 23.0 %collective-permute-start.41 = (bf16[24,6144]{1,0:T(8,128)(2,1)S(1)}, bf16[24,6144]{1,0:T(8,128)(2,1)S(1)}, u32[]{:S(2)}, u32[]{:S(2)}) collective-permute-start(bf16[24,6144]{1,0:T(8,128)(2,1)S(1)} %get-tuple-element.240), channel_id=1, source_target_pairs={{0,24},{1,25},{2,26},{3,27},{4,28},{5,29},{6,30},{7,31},{8,16},{9,... | collective-permute-start | bytes 884744 | tf_op jit(solution)/shard_map/ppermute | solution.py:402
  217.1 13.6 %collective-permute-start.42 = (bf16[24,3072]{1,0:T(8,128)(2,1)S(1)}, bf16[24,3072]{1,0:T(8,128)(2,1)S(1)}, u32[]{:S(2)}, u32[]{:S(2)}) collective-permute-start(bf16[24,3072]{1,0:T(8,128)(2,1)S(1)} %get-tuple-element.242), channel_id=1, source_target_pairs={{0,8},{1,9},{2,10},{3,11},{4,12},{5,13},{6,14},{7,15},{8,0},{9,1},... | collective-permute-start | bytes 442376 | tf_op jit(solution)/shard_map/ppermute | solution.py:402
  221.0 17.7 %collective-permute-start.43 = (bf16[24,3072]{1,0:T(8,128)(2,1)S(1)}, bf16[24,3072]{1,0:T(8,128)(2,1)S(1)}, u32[]{:S(2)}, u32[]{:S(2)}) collective-permute-start(bf16[24,3072]{1,0:T(8,128)(2,1)S(1)} %get-tuple-element.243), channel_id=1, source_target_pairs={{0,16},{1,17},{2,18},{3,19},{4,20},{5,21},{6,22},{7,23},{8,24},{9,... | collective-permute-start | bytes 442376 | tf_op jit(solution)/shard_map/ppermute | solution.py:402
  221.5 17.2 %collective-permute-start.44 = (bf16[24,3072]{1,0:T(8,128)(2,1)S(1)}, bf16[24,3072]{1,0:T(8,128)(2,1)S(1)}, u32[]{:S(2)}, u32[]{:S(2)}) collective-permute-start(bf16[24,3072]{1,0:T(8,128)(2,1)S(1)} %get-tuple-element.244), channel_id=1, source_target_pairs={{0,24},{1,25},{2,26},{3,27},{4,28},{5,29},{6,30},{7,31},{8,16},{9,... | collective-permute-start | bytes 442376 | tf_op jit(solution)/shard_map/ppermute | solution.py:402
  (53 other events, 610.2 us)

commit v2 on v1

--- a/solution.py
+++ b/solution.py
@@ -321,17 +321,13 @@
             put(0, j, dot_tn(s, k2) * factor)
 
 
-def weight_kernel(sc, n1, att, pg, b1g, go, gs, n1t):
+def weight_kernel(sc, n1, att, pg, b1g, go, gs):
     step = pl.program_id(0)
     last = pl.num_programs(0) - 1
 
-    @pl.when(step == 0)
-    def _():
-        n1t[...] = n1[...].T
-
     @pl.when(step < last)
     def _():
-        part(sc[0], dot(n1t[...], pg[...]).astype(BF16), go, gs)
+        part(sc[0], dot_tn(n1[...], pg[...]).astype(BF16), go, gs)
 
     @pl.when(step == last)
     def _():
@@ -819,10 +815,29 @@
         (sc,),
         [(n1, whole), (att, whole), (pg, pl.BlockSpec((rows, width), lambda i, *_: (0, jnp.minimum(i, 2)))), (b1g, whole)],
         [((COLUMNS, thin, 4 * width), BF16, column_blocks)] * 2,
-        [turned_scr],
+        (),
         chain,
         mib=18,
     )
+    per = pack // tile
+    input_grad, input_sums, token = call(
+        partial(input_back_kernel, images=images),
+        (rows // tile,),
+        (grid_flat, sc),
+        [(pg, by_tile(3 * width)), (qp_own, qkv_blocks), (qp_other, qkv_blocks)]
+        + [(x, by_tile(width)), (far(mg), by_tile(width)), (norm_gain, vec2)],
+        [((rows, width), F32, pl.BlockSpec((pack, width), lambda i, *_: (i // per, 0)), "far"), ((2, width), F32, vec2)],
+        [qkv_scr, pltpu.VMEM((tile, width), F32)] + [pltpu.VMEM((pack, width), BF16)] * 2,
+        [token],
+        mib=24,
+    )
+
+    chain = []
+    if swaps:
+        qp_parts, token = fold_core(qp_grad_own, qp_grad_other, sc, [token])
+        token, fc_parts = fold_sends(fold_second(fc_parts, sc, [token]))
+        chain = [token]
+
     layer_out, out_sums, token = call(
         partial(layer_out_kernel, images=images, tiles=tiles),
         (tiles + packs,),
@@ -831,28 +846,9 @@
         + [(layer_scale, vec2), (fc2_bias[None], vec1)],
         [((rows, width), BF16, then(pack), "far"), ((1, width), F32, vec1)],
         [sum_scr, pltpu.VMEM((pack, width), BF16), fc2_scr],
-        [token],
+        chain,
         mib=26,
     )
-    chain = []
-    if swaps:
-        qp_parts, token = fold_core(qp_grad_own, qp_grad_other, sc, [token])
-        token, fc_parts = fold_sends(fold_second(fc_parts, sc, [token]))
-        chain = [token]
-
-    per = pack // tile
-    input_grad, input_sums, token = call(
-        partial(input_back_kernel, images=images),
-        (rows // tile,),
-        (grid_flat, sc),
-        [(pg, by_tile(3 * width)), (qp_own, qkv_blocks), (qp_other, qkv_blocks)]
-        + [(x, by_tile(width)), (mg, by_tile(width)), (norm_gain, vec2)],
-        [((rows, width), F32, pl.BlockSpec((pack, width), lambda i, *_: (i // per, 0)), "far"), ((2, width), F32, vec2)],
-        [qkv_scr, pltpu.VMEM((tile, width), F32)] + [pltpu.VMEM((pack, width), BF16)] * 2,
-        chain,
-        mib=24,
-    )
-
     chain = []
     if swaps:
         qp_parts, token = fold_first(qp_parts, sc, [token, fc_parts[1]])

time: 241 us -> 239 us (level)
  transfers between devices with their start and end apart: 49 -> 49, of which waited for: 21 -> 20; matrix products, arithmetic and copies ran while one was open for 0% -> 0% of each run, Pallas kernels for 47% -> 48%
where the time goes in v2:
time: 239 us
  Pallas kernels  136 us (57%)
  starting transfers between devices  58 us (24%)
  waiting for transfers between devices  40.7 us (17%)
  local copies, waits for them, and re-layouts  2.79 us (1%)
    pallas_call x34, Pallas kernels, call(): pl.pallas_call(run, grid_spec=pltpu.PrefetchScalarGridSpec(num_scalar_pre...  136 us
    ppermute x49, starting transfers between devices, swap(): return lax.ppermute(v, AXES, [(i, i ^ mask) for i in range(32)])  58 us
    ppermute x49, waiting for transfers between devices, swap(): return lax.ppermute(v, AXES, [(i, i ^ mask) for i in range(32)])  40.7 us
  transfers between devices with their start and end apart: 49, of which 20 were waited for; matrix products, arithmetic and copies ran while one was open for 0% of the time, Pallas kernels for 48%

profile of v2, /device:TPU:0, one launch (start us, length us, event | category | flops | bytes accessed | tf_op | source)
XLA Modules:
  0.0 239.0 jit_solution(3160965885699145575)
XLA Ops:
  2.4 3.0 %collective-permute-start = (bf16[24,3072]{1,0:T(8,128)(2,1)S(1)}, bf16[24,3072]{1,0:T(8,128)(2,1)S(1)}, u32[]{:S(2)}, u32[]{:S(2)}) collective-permute-start(bf16[24,3072]{1,0:T(8,128)(2,1)S(1)} %get-tuple-element.138.refs_1_), channel_id=1, source_target_pairs={{0,8},{1,9},{2,10},{3,11},{4,12},{5,13},{6,14},{7,15},{8,0},{9,1},... | collective-permute-start | bytes 442376 | tf_op jit(solution)/shard_map/ppermute | solution.py:398
  5.4 2.6 %collective-permute-start.1 = (bf16[24,3072]{1,0:T(8,128)(2,1)S(1)}, bf16[24,3072]{1,0:T(8,128)(2,1)S(1)}, u32[]{:S(2)}, u32[]{:S(2)}) collective-permute-start(bf16[24,3072]{1,0:T(8,128)(2,1)S(1)} %get-tuple-element.138.refs_1_), channel_id=1, source_target_pairs={{0,16},{1,17},{2,18},{3,19},{4,20},{5,21},{6,22},{7,23},{8,24},{9,... | collective-permute-start | bytes 442376 | tf_op jit(solution)/shard_map/ppermute | solution.py:398
  14.0 5.3 %collective-permute-done.1.refs_3_ = bf16[24,3072]{1,0:T(8,128)(2,1)S(1)} collective-permute-done((bf16[24,3072]{1,0:T(8,128)(2,1)S(1)}, bf16[24,3072]{1,0:T(8,128)(2,1)S(1)}, u32[]{:S(2)}, u32[]{:S(2)}) %collective-permute-start.1) | collective-permute-done | bytes 147488 | tf_op jit(solution)/shard_map/ppermute | solution.py:398
  25.9 2.5 %collective-permute-start.8 = (bf16[24,3072]{1,0:T(8,128)(2,1)S(1)}, bf16[24,3072]{1,0:T(8,128)(2,1)S(1)}, u32[]{:S(2)}, u32[]{:S(2)}) collective-permute-start(bf16[24,3072]{1,0:T(8,128)(2,1)S(1)} %get-tuple-element.143.refs_1_), channel_id=1, source_target_pairs={{0,24},{1,25},{2,26},{3,27},{4,28},{5,29},{6,30},{7,31},{8,16},{9,... | collective-permute-start | bytes 442376 | tf_op jit(solution)/shard_map/ppermute | solution.py:398
  30.3 3.2 %collective-permute-done.8.refs_6_.refs_4_ = bf16[24,3072]{1,0:T(8,128)(2,1)S(1)} collective-permute-done((bf16[24,3072]{1,0:T(8,128)(2,1)S(1)}, bf16[24,3072]{1,0:T(8,128)(2,1)S(1)}, u32[]{:S(2)}, u32[]{:S(2)}) %collective-permute-start.8) | collective-permute-done | bytes 147488 | tf_op jit(solution)/shard_map/ppermute | solution.py:398
  35.3 2.6 %collective-permute-start.11 = (bf16[24,3072]{1,0:T(8,128)(2,1)S(1)}, bf16[24,3072]{1,0:T(8,128)(2,1)S(1)}, u32[]{:S(2)}, u32[]{:S(2)}) collective-permute-start(bf16[24,3072]{1,0:T(8,128)(2,1)S(1)} %get-tuple-element.143.refs_1_), channel_id=1, source_target_pairs={{0,16},{1,17},{2,18},{3,19},{4,20},{5,21},{6,22},{7,23},{8,24},{9,... | collective-permute-start | bytes 442376 | tf_op jit(solution)/shard_map/ppermute | solution.py:398
  38.2 7.7 %shard_map.240 = (bf16[1024,768]{1,0:T(8,128)(2,1)}, bf16[1024,768]{1,0:T(8,128)(2,1)}, bf16[1024,768]{1,0:T(8,128)(2,1)}, bf16[1024,768]{1,0:T(8,128)(2,1)}, f3...) custom-call(s32[16]{0:T(128)S(1)} %reshape.65.refs_0_, bf16[1024,768]{1,0:T(8,128)(2,1)} %refs_1_.3, bf16[1024,768]{1,0:T(8,128)(2,1)} %refs_2_.3, ...), custom_call_target="tpu_custom_call" | custom-call | flops 1 | bytes 1 | tf_op jit(solution)/shard_map/pallas_call | solution.py:44
  47.4 2.3 shard_map.242
  54.3 10.5 %shard_map.243 = (bf16[1024,2304]{1,0:T(8,128)(2,1)}, bf16[1024,768]{1,0:T(8,128)(2,1)S(1)}, f32[96,128]{1,0:T(8,128)S(1)}, f32[8,128]{1,0:T(8,128)S(1)}) custom-call(s32[16]{0:T(128)S(1)} %reshape.65.refs_0_, s32[4]{0:T(128)S(1)} %pad_add_fusion.refs_0_.refs_1_, bf16[1024,768]{1,0:T(8,128)(2,1)} %get-tuple-element.145.refs_2_.refs_1_, ...), custom_call_target="tpu_custom_call" | custom-call | flops 1 | bytes 1 | tf_op jit(solution)/shard_map/pallas_call | solution.py:44
  71.2 4.3 %shard_map.245 = (f32[1024,768]{1,0:T(8,128)}, bf16[1024,768]{1,0:T(8,128)(2,1)S(1)}, f32[8,128]{1,0:T(8,128)S(1)}) custom-call(s32[4]{0:T(128)S(1)} %pad_add_fusion.refs_0_.refs_1_, bf16[1024,768]{1,0:T(8,128)(2,1)S(1)} %get-tuple-element.153.refs_1_.refs_2_, bf16[1024,768]{1,0:T(8,128)(2,1)S(1)} %copy-done, f32[2,768]{1,0:T(2,128)S(1)} %copy-done.14, ...), custom_call_target="tpu_custom_call" | custom-call | flops 1 | bytes 1 | tf_op jit(solution)/shard_map/pallas_call | solution.py:44
  75.6 4.2 %collective-permute-done.19.refs_4_ = bf16[2,2,24,1536]{3,2,1,0:T(8,128)(2,1)S(1)} collective-permute-done((bf16[2,2,24,1536]{3,2,1,0:T(8,128)(2,1)S(1)}, bf16[2,2,24,1536]{3,2,1,0:T(8,128)(2,1)S(1)}, u32[]{:S(2)}, u32[]{:S(2)}) %collective-permute-start.19) | collective-permute-done | bytes 294944 | tf_op jit(solution)/shard_map/ppermute | solution.py:398
  83.8 2.3 shard_map.247
  90.7 12.0 %shard_map.248 = (bf16[1024,3072]{1,0:T(8,128)(2,1)}, f32[1024,3072]{1,0:T(8,128)}, bf16[8,192,768]{2,1,0:T(8,128)(2,1)}, bf16[8,192,768]{2,1,0:T(8,128)(2,1)}, f32[8,128]{1,0:T(8,128)S(1)}) custom-call(s32[4]{0:T(128)S(1)} %pad_add_fusion.refs_0_.refs_1_, bf16[1024,768]{1,0:T(8,128)(2,1)S(1)} %get-tuple-element.159.refs_1_.refs_2_, ...), custom_call_target="tpu_custom_call" | custom-call | flops 1 | bytes 1 | tf_op jit(solution)/shard_map/pallas_call | solution.py:44
  106.3 5.2 %shard_map.250 = (bf16[1024,3072]{1,0:T(8,128)(2,1)}, f32[1024,3072]{1,0:T(8,128)}, bf16[8,192,768]{2,1,0:T(8,128)(2,1)}, bf16[8,192,768]{2,1,0:T(8,128)(2,1)}, f32[8,128]{1,0:T(8,128)}) custom-call(s32[4]{0:T(128)S(1)} %pad_add_fusion.refs_0_.refs_1_, ...), custom_call_target="tpu_custom_call", output_to_operand_aliasing={{0}: (6, {}), {1}: (7, {}), {2}: (8, {}), {3}: (9, {})} | custom-call | flops 1 | bytes 1 | tf_op jit(solution)/shard_map/pallas_call | solution.py:44
  111.9 15.7 %shard_map.251 = (bf16[1024,3072]{1,0:T(8,128)(2,1)}, f32[1,3072]{1,0:T(1,128)S(1)}, bf16[8,48,3072]{2,1,0:T(8,128)(2,1)}, bf16[8,48,3072]{2,1,0:T(8,128)(2,1)}, f32[8,128]{1,0:T(8,128)S(1)}) custom-call(s32[4]{0:T(128)S(1)} %pad_add_fusion.refs_0_.refs_1_, bf16[1024,768]{1,0:T(8,128)(2,1)} %get-tuple-element.160.refs_2_.refs_1_, ...), custom_call_target="tpu_custom_call" | custom-call | flops 1 | bytes 1 | tf_op jit(solution)/shard_map/pallas_call | solution.py:44
  131.3 14.8 %shard_map.253 = (f32[1024,768]{1,0:T(8,128)}, bf16[1024,768]{1,0:T(8,128)(2,1)S(1)}, bf16[1024,768]{1,0:T(8,128)(2,1)S(1)}, f32[4,768]{1,0:T(4,128)S(1)}, f32[8,128]{1,0:T(8,128)S(1)}) custom-call(s32[4]{0:T(128)S(1)} %pad_add_fusion.refs_0_.refs_1_, bf16[1024,3072]{1,0:T(8,128)(2,1)} %get-tuple-element.182.refs_1_, bf16[8,48,3072]{2,1,0:T(8,128)(2,1)S(1)} %bitcast.27, ...), custom_call_target="tpu_custom_call" | custom-call | flops 1 | bytes 1 | tf_op jit(solution)/shard_map/pallas_call | solution.py:44
  149.1 12.8 %shard_map.255 = (bf16[1024,2304]{1,0:T(8,128)(2,1)S(1)}, f32[8,2304]{1,0:T(8,128)S(1)}, f32[8,128]{1,0:T(8,128)S(1)}) custom-call(s32[16]{0:T(128)S(1)} %reshape.65.refs_0_, bf16[1024,2304]{1,0:T(8,128)(2,1)} %get-tuple-element.196.refs_1_, bf16[1024,768]{1,0:T(8,128)(2,1)S(1)} %get-tuple-element.197.refs_2_, f32[96,128]{1,0:T(8,128)S(1)} %get-tuple-element.198.refs_3_, ...), custom_call_target="tpu_custom_call" | custom-call | flops 1 | bytes 1 | tf_op jit(solution)/shard_map/pallas_call | solution.py:44
  164.8 7.3 %shard_map.257 = (bf16[8,48,3072]{2,1,0:T(8,128)(2,1)S(1)}, bf16[8,48,3072]{2,1,0:T(8,128)(2,1)S(1)}, f32[8,128]{1,0:T(8,128)S(1)}) custom-call(s32[4]{0:T(128)S(1)} %pad_add_fusion.refs_0_.refs_1_, bf16[1024,768]{1,0:T(8,128)(2,1)S(1)} %copy-done.5, bf16[1024,768]{1,0:T(8,128)(2,1)S(1)} %get-tuple-element.153.refs_1_.refs_2_, ...), custom_call_target="tpu_custom_call" | custom-call | flops 1 | bytes 1 | tf_op jit(solution)/shard_map/pallas_call | solution.py:44
  173.9 11.2 %shard_map.258 = (f32[1024,768]{1,0:T(8,128)}, f32[2,768]{1,0:T(2,128)S(1)}, f32[8,128]{1,0:T(8,128)S(1)}) custom-call(s32[16]{0:T(128)S(1)} %reshape.65.refs_0_, s32[4]{0:T(128)S(1)} %pad_add_fusion.refs_0_.refs_1_, bf16[1024,2304]{1,0:T(8,128)(2,1)S(1)} %get-tuple-element.205.refs_3_.refs_2_, bf16[8,48,3072]{2,1,0:T(8,128)(2,1)S(1)} %bitcast.20, ...), custom_call_target="tpu_custom_call" | custom-call | flops 1 | bytes 1 | tf_op jit(solution)/shard_map/pallas_call | solution.py:44
  194.0 11.1 %shard_map.261 = (bf16[1024,768]{1,0:T(8,128)(2,1)}, f32[1,768]{1,0:T(1,128)S(1)}, f32[8,128]{1,0:T(8,128)S(1)}) custom-call(s32[16]{0:T(128)S(1)} %reshape.65.refs_0_, s32[4]{0:T(128)S(1)} %pad_add_fusion.refs_0_.refs_1_, bf16[1024,3072]{1,0:T(8,128)(2,1)} %get-tuple-element.175.refs_2_, bf16[8,192,768]{2,1,0:T(8,128)(2,1)S(1)} %bitcast.32, ...), custom_call_target="tpu_custom_call" | custom-call | flops 1 | bytes 1 | tf_op jit(solution)/shard_map/pallas_call | solution.py:44
  210.9 4.2 %collective-permute-done.39.refs_2_ = f32[14,768]{1,0:T(8,128)S(1)} collective-permute-done((f32[14,768]{1,0:T(8,128)S(1)}, f32[14,768]{1,0:T(8,128)S(1)}, u32[]{:S(2)}, u32[]{:S(2)}) %collective-permute-start.39) | collective-permute-done | bytes 43040 | tf_op jit(solution)/shard_map/ppermute | solution.py:398
  216.4 3.0 %collective-permute-start.42 = (bf16[24,3072]{1,0:T(8,128)(2,1)S(1)}, bf16[24,3072]{1,0:T(8,128)(2,1)S(1)}, u32[]{:S(2)}, u32[]{:S(2)}) collective-permute-start(bf16[24,3072]{1,0:T(8,128)(2,1)S(1)} %get-tuple-element.242), channel_id=1, source_target_pairs={{0,8},{1,9},{2,10},{3,11},{4,12},{5,13},{6,14},{7,15},{8,0},{9,1},... | collective-permute-start | bytes 442376 | tf_op jit(solution)/shard_map/ppermute | solution.py:398
  222.9 3.0 %collective-permute-done.45.refs_2_ = f32[14,768]{1,0:T(8,128)S(1)} collective-permute-done((f32[14,768]{1,0:T(8,128)S(1)}, f32[14,768]{1,0:T(8,128)S(1)}, u32[]{:S(2)}, u32[]{:S(2)}) %collective-permute-start.45) | collective-permute-done | bytes 43040 | tf_op jit(solution)/shard_map/ppermute | solution.py:398
  232.2 4.8 %collective-permute-done.47.refs_3_ = f32[14,768]{1,0:T(8,128)S(1)} collective-permute-done((f32[14,768]{1,0:T(8,128)S(1)}, f32[14,768]{1,0:T(8,128)S(1)}, u32[]{:S(2)}, u32[]{:S(2)}) %collective-permute-start.47) | collective-permute-done | bytes 43040 | tf_op jit(solution)/shard_map/ppermute | solution.py:398
  (171 shorter events, 82.3 us)
Async XLA Ops:
  5.4 14.0 %collective-permute-start.1 = (bf16[24,3072]{1,0:T(8,128)(2,1)S(1)}, bf16[24,3072]{1,0:T(8,128)(2,1)S(1)}, u32[]{:S(2)}, u32[]{:S(2)}) collective-permute-start(bf16[24,3072]{1,0:T(8,128)(2,1)S(1)} %get-tuple-element.138.refs_1_), channel_id=1, source_target_pairs={{0,16},{1,17},{2,18},{3,19},{4,20},{5,21},{6,22},{7,23},{8,24},{9,... | collective-permute-start | bytes 442376 | tf_op jit(solution)/shard_map/ppermute | solution.py:398
  49.8 16.6 %collective-permute-start.16 = (bf16[2,2,24,1536]{3,2,1,0:T(8,128)(2,1)S(1)}, bf16[2,2,24,1536]{3,2,1,0:T(8,128)(2,1)S(1)}, u32[]{:S(2)}, u32[]{:S(2)}) collective-permute-start(bf16[2,2,24,1536]{3,2,1,0:T(8,128)(2,1)S(1)} %get-tuple-element.149.refs_1_), channel_id=1, source_target_pairs={{0,16},{1,17},{2,18},{3,19},{4,20},{5,21},{6,22},{7,23},{8,24},{9,... | collective-permute-start | bytes 884744 | tf_op jit(solution)/shard_map/ppermute | solution.py:398
  50.0 16.4 %collective-permute-start.14 = (bf16[4,24,1536]{2,1,0:T(8,128)(2,1)S(1)}, bf16[4,24,1536]{2,1,0:T(8,128)(2,1)S(1)}, u32[]{:S(2)}, u32[]{:S(2)}) collective-permute-start(bf16[4,24,1536]{2,1,0:T(8,128)(2,1)S(1)} %get-tuple-element.155.refs_1_), channel_id=1, source_target_pairs={{0,4},{1,5},{2,6},{3,7},{4,0},{5,1},{6,2},{7,3},{8,12},{9,13},{10,... | collective-permute-start | bytes 884744 | tf_op jit(solution)/shard_map/ppermute | solution.py:398
  51.5 14.9 %collective-permute-start.15 = (bf16[4,24,1536]{2,1,0:T(8,128)(2,1)S(1)}, bf16[4,24,1536]{2,1,0:T(8,128)(2,1)S(1)}, u32[]{:S(2)}, u32[]{:S(2)}) collective-permute-start(bf16[4,24,1536]{2,1,0:T(8,128)(2,1)S(1)} %get-tuple-element.156.refs_3_), channel_id=1, source_target_pairs={{0,1},{1,0},{2,3},{3,2},{4,5},{5,4},{6,7},{7,6},{8,9},{9,8},{10,11... | collective-permute-start | bytes 884744 | tf_op jit(solution)/shard_map/ppermute | solution.py:398
  67.1 15.3 %collective-permute-start.17 = (bf16[2,4,24,1536]{3,2,1,0:T(8,128)(2,1)S(1)}, bf16[2,4,24,1536]{3,2,1,0:T(8,128)(2,1)S(1)}, u32[]{:S(2)}, u32[]{:S(2)}) collective-permute-start(bf16[2,4,24,1536]{3,2,1,0:T(8,128)(2,1)S(1)} %get-tuple-element.161.refs_1_), channel_id=1, source_target_pairs={{0,1},{1,0},{2,3},{3,2},{4,5},{5,4},{6,7},{7,6},{8,9},{9,8},{10,11... | collective-permute-start | bytes 1769480 | tf_op jit(solution)/shard_map/ppermute | solution.py:398
  68.0 15.0 %collective-permute-start.18 = (bf16[2,4,24,1536]{3,2,1,0:T(8,128)(2,1)S(1)}, bf16[2,4,24,1536]{3,2,1,0:T(8,128)(2,1)S(1)}, u32[]{:S(2)}, u32[]{:S(2)}) collective-permute-start(bf16[2,4,24,1536]{3,2,1,0:T(8,128)(2,1)S(1)} %get-tuple-element.162.refs_3_), channel_id=1, source_target_pairs={{0,4},{1,5},{2,6},{3,7},{4,0},{5,1},{6,2},{7,3},{8,12},{9,13},{10,... | collective-permute-start | bytes 1769480 | tf_op jit(solution)/shard_map/ppermute | solution.py:398
  86.2 16.6 %collective-permute-start.21 = (bf16[2,4,24,1536]{3,2,1,0:T(8,128)(2,1)S(1)}, bf16[2,4,24,1536]{3,2,1,0:T(8,128)(2,1)S(1)}, u32[]{:S(2)}, u32[]{:S(2)}) collective-permute-start(bf16[2,4,24,1536]{3,2,1,0:T(8,128)(2,1)S(1)} %get-tuple-element.171.refs_1_), channel_id=1, source_target_pairs={{0,1},{1,0},{2,3},{3,2},{4,5},{5,4},{6,7},{7,6},{8,9},{9,8},{10,11... | collective-permute-start | bytes 1769480 | tf_op jit(solution)/shard_map/ppermute | solution.py:398
  87.4 15.4 %collective-permute-start.22 = (bf16[2,4,24,1536]{3,2,1,0:T(8,128)(2,1)S(1)}, bf16[2,4,24,1536]{3,2,1,0:T(8,128)(2,1)S(1)}, u32[]{:S(2)}, u32[]{:S(2)}) collective-permute-start(bf16[2,4,24,1536]{3,2,1,0:T(8,128)(2,1)S(1)} %get-tuple-element.172.refs_3_), channel_id=1, source_target_pairs={{0,4},{1,5},{2,6},{3,7},{4,0},{5,1},{6,2},{7,3},{8,12},{9,13},{10,... | collective-permute-start | bytes 1769480 | tf_op jit(solution)/shard_map/ppermute | solution.py:398
  111.5 16.2 %collective-permute-start.25 = (bf16[8,192,768]{2,1,0:T(8,128)(2,1)}, bf16[8,192,768]{2,1,0:T(8,128)(2,1)S(1)}, u32[]{:S(2)}, u32[]{:S(2)}) collective-permute-start(bf16[8,192,768]{2,1,0:T(8,128)(2,1)} %get-tuple-element.184), channel_id=1, source_target_pairs={{0,2},{1,3},{2,0},{3,1},{4,6},{5,7},{6,4},{7,5},{8,10},{9,11},{10,... | collective-permute-start | bytes 7077896 | tf_op jit(solution)/shard_map/ppermute | solution.py:398
  127.6 18.6 %collective-permute-start.24 = (bf16[8,48,3072]{2,1,0:T(8,128)(2,1)}, bf16[8,48,3072]{2,1,0:T(8,128)(2,1)S(1)}, u32[]{:S(2)}, u32[]{:S(2)}) collective-permute-start(bf16[8,48,3072]{2,1,0:T(8,128)(2,1)} %get-tuple-element.181), channel_id=1, source_target_pairs={{0,2},{1,3},{2,0},{3,1},{4,6},{5,7},{6,4},{7,5},{8,10},{9,11},{10,... | collective-permute-start | bytes 7077896 | tf_op jit(solution)/shard_map/ppermute | solution.py:398
  128.9 33.0 %collective-permute-start.27 = (bf16[4,2,96,384]{3,2,1,0:T(8,128)(2,1)S(1)}, bf16[4,2,96,384]{3,2,1,0:T(8,128)(2,1)S(1)}, u32[]{:S(2)}, u32[]{:S(2)}) collective-permute-start(bf16[4,2,96,384]{3,2,1,0:T(8,128)(2,1)S(1)} %get-tuple-element.191), channel_id=1, source_target_pairs={{0,1},{1,0},{2,3},{3,2},{4,5},{5,4},{6,7},{7,6},{8,9},{9,8},{10,11... | collective-permute-start | bytes 1769480 | tf_op jit(solution)/shard_map/ppermute | solution.py:398
  130.1 31.8 %collective-permute-start.29 = (bf16[4,2,96,384]{3,2,1,0:T(8,128)(2,1)S(1)}, bf16[4,2,96,384]{3,2,1,0:T(8,128)(2,1)S(1)}, u32[]{:S(2)}, u32[]{:S(2)}) collective-permute-start(bf16[4,2,96,384]{3,2,1,0:T(8,128)(2,1)S(1)} %get-tuple-element.195), channel_id=1, source_target_pairs={{0,4},{1,5},{2,6},{3,7},{4,0},{5,1},{6,2},{7,3},{8,12},{9,13},{10,... | collective-permute-start | bytes 1769480 | tf_op jit(solution)/shard_map/ppermute | solution.py:398
  147.4 15.1 %collective-permute-start.26 = (bf16[4,2,24,1536]{3,2,1,0:T(8,128)(2,1)S(1)}, bf16[4,2,24,1536]{3,2,1,0:T(8,128)(2,1)S(1)}, u32[]{:S(2)}, u32[]{:S(2)}) collective-permute-start(bf16[4,2,24,1536]{3,2,1,0:T(8,128)(2,1)S(1)} %get-tuple-element.189), channel_id=1, source_target_pairs={{0,1},{1,0},{2,3},{3,2},{4,5},{5,4},{6,7},{7,6},{8,9},{9,8},{10,11... | collective-permute-start | bytes 1769480 | tf_op jit(solution)/shard_map/ppermute | solution.py:398
  148.6 14.7 %collective-permute-start.28 = (bf16[4,2,24,1536]{3,2,1,0:T(8,128)(2,1)S(1)}, bf16[4,2,24,1536]{3,2,1,0:T(8,128)(2,1)S(1)}, u32[]{:S(2)}, u32[]{:S(2)}) collective-permute-start(bf16[4,2,24,1536]{3,2,1,0:T(8,128)(2,1)S(1)} %get-tuple-element.193), channel_id=1, source_target_pairs={{0,4},{1,5},{2,6},{3,7},{4,0},{5,1},{6,2},{7,3},{8,12},{9,13},{10,... | collective-permute-start | bytes 1769480 | tf_op jit(solution)/shard_map/ppermute | solution.py:398
  172.0 13.1 %collective-permute-start.32 = (bf16[8,48,3072]{2,1,0:T(8,128)(2,1)S(1)}, bf16[8,48,3072]{2,1,0:T(8,128)(2,1)S(1)}, u32[]{:S(2)}, u32[]{:S(2)}) collective-permute-start(bf16[8,48,3072]{2,1,0:T(8,128)(2,1)S(1)} %get-tuple-element.209), channel_id=1, source_target_pairs={{0,2},{1,3},{2,0},{3,1},{4,6},{5,7},{6,4},{7,5},{8,10},{9,11},{10,... | collective-permute-start | bytes 7077896 | tf_op jit(solution)/shard_map/ppermute | solution.py:398
  172.1 16.6 %collective-permute-start.30 = (bf16[4,24,3072]{2,1,0:T(8,128)(2,1)S(1)}, bf16[4,24,3072]{2,1,0:T(8,128)(2,1)S(1)}, u32[]{:S(2)}, u32[]{:S(2)}) collective-permute-start(bf16[4,24,3072]{2,1,0:T(8,128)(2,1)S(1)} %get-tuple-element.202), channel_id=1, source_target_pairs={{0,4},{1,5},{2,6},{3,7},{4,0},{5,1},{6,2},{7,3},{8,12},{9,13},{10,... | collective-permute-start | bytes 1769480 | tf_op jit(solution)/shard_map/ppermute | solution.py:398
  172.7 16.0 %collective-permute-start.31 = (bf16[4,24,3072]{2,1,0:T(8,128)(2,1)S(1)}, bf16[4,24,3072]{2,1,0:T(8,128)(2,1)S(1)}, u32[]{:S(2)}, u32[]{:S(2)}) collective-permute-start(bf16[4,24,3072]{2,1,0:T(8,128)(2,1)S(1)} %get-tuple-element.204), channel_id=1, source_target_pairs={{0,1},{1,0},{2,3},{3,2},{4,5},{5,4},{6,7},{7,6},{8,9},{9,8},{10,11... | collective-permute-start | bytes 1769480 | tf_op jit(solution)/shard_map/ppermute | solution.py:398
  186.3 18.8 %collective-permute-start.33 = (bf16[4,2,24,1536]{3,2,1,0:T(8,128)(2,1)S(1)}, bf16[4,2,24,1536]{3,2,1,0:T(8,128)(2,1)S(1)}, u32[]{:S(2)}, u32[]{:S(2)}) collective-permute-start(bf16[4,2,24,1536]{3,2,1,0:T(8,128)(2,1)S(1)} %get-tuple-element.218), channel_id=1, source_target_pairs={{0,1},{1,0},{2,3},{3,2},{4,5},{5,4},{6,7},{7,6},{8,9},{9,8},{10,11... | collective-permute-start | bytes 1769480 | tf_op jit(solution)/shard_map/ppermute | solution.py:398
  187.2 17.8 %collective-permute-start.34 = (bf16[4,2,24,1536]{3,2,1,0:T(8,128)(2,1)S(1)}, bf16[4,2,24,1536]{3,2,1,0:T(8,128)(2,1)S(1)}, u32[]{:S(2)}, u32[]{:S(2)}) collective-permute-start(bf16[4,2,24,1536]{3,2,1,0:T(8,128)(2,1)S(1)} %get-tuple-element.220), channel_id=1, source_target_pairs={{0,4},{1,5},{2,6},{3,7},{4,0},{5,1},{6,2},{7,3},{8,12},{9,13},{10,... | collective-permute-start | bytes 1769480 | tf_op jit(solution)/shard_map/ppermute | solution.py:398
  189.5 15.5 %collective-permute-start.35 = (bf16[24,6144]{1,0:T(8,128)(2,1)S(1)}, bf16[24,6144]{1,0:T(8,128)(2,1)S(1)}, u32[]{:S(2)}, u32[]{:S(2)}) collective-permute-start(bf16[24,6144]{1,0:T(8,128)(2,1)S(1)} %get-tuple-element.222), channel_id=1, source_target_pairs={{0,8},{1,9},{2,10},{3,11},{4,12},{5,13},{6,14},{7,15},{8,0},{9,1},... | collective-permute-start | bytes 884744 | tf_op jit(solution)/shard_map/ppermute | solution.py:398
  190.2 25.5 %collective-permute-start.40 = (bf16[24,6144]{1,0:T(8,128)(2,1)S(1)}, bf16[24,6144]{1,0:T(8,128)(2,1)S(1)}, u32[]{:S(2)}, u32[]{:S(2)}) collective-permute-start(bf16[24,6144]{1,0:T(8,128)(2,1)S(1)} %get-tuple-element.239), channel_id=1, source_target_pairs={{0,16},{1,17},{2,18},{3,19},{4,20},{5,21},{6,22},{7,23},{8,24},{9,... | collective-permute-start | bytes 884744 | tf_op jit(solution)/shard_map/ppermute | solution.py:398
  191.9 23.7 %collective-permute-start.41 = (bf16[24,6144]{1,0:T(8,128)(2,1)S(1)}, bf16[24,6144]{1,0:T(8,128)(2,1)S(1)}, u32[]{:S(2)}, u32[]{:S(2)}) collective-permute-start(bf16[24,6144]{1,0:T(8,128)(2,1)S(1)} %get-tuple-element.240), channel_id=1, source_target_pairs={{0,24},{1,25},{2,26},{3,27},{4,28},{5,29},{6,30},{7,31},{8,16},{9,... | collective-permute-start | bytes 884744 | tf_op jit(solution)/shard_map/ppermute | solution.py:398
  219.4 17.7 %collective-permute-start.43 = (bf16[24,3072]{1,0:T(8,128)(2,1)S(1)}, bf16[24,3072]{1,0:T(8,128)(2,1)S(1)}, u32[]{:S(2)}, u32[]{:S(2)}) collective-permute-start(bf16[24,3072]{1,0:T(8,128)(2,1)S(1)} %get-tuple-element.243), channel_id=1, source_target_pairs={{0,16},{1,17},{2,18},{3,19},{4,20},{5,21},{6,22},{7,23},{8,24},{9,... | collective-permute-start | bytes 442376 | tf_op jit(solution)/shard_map/ppermute | solution.py:398
  219.9 17.1 %collective-permute-start.44 = (bf16[24,3072]{1,0:T(8,128)(2,1)S(1)}, bf16[24,3072]{1,0:T(8,128)(2,1)S(1)}, u32[]{:S(2)}, u32[]{:S(2)}) collective-permute-start(bf16[24,3072]{1,0:T(8,128)(2,1)S(1)} %get-tuple-element.244), channel_id=1, source_target_pairs={{0,24},{1,25},{2,26},{3,27},{4,28},{5,29},{6,30},{7,31},{8,16},{9,... | collective-permute-start | bytes 442376 | tf_op jit(solution)/shard_map/ppermute | solution.py:398
  (52 other events, 593.3 us)

commit v3 on v2

--- a/solution.py
+++ b/solution.py
@@ -490,7 +490,7 @@
                             pairs.append((sides[j].at[i, k, :, pl.ds(r * width, width)], to.at[pl.ds(run * rows, rows)]))
         return pairs
 
-    ins = [far(v) for v in (left, swap(left, Y), right, swap(right, X))]
+    ins = [left, swap(left, Y), right, swap(right, X)]
     own, token = move(plan, sc, ins, [(4, 2, 2, runs * rows, width)], after, 12)
     shape = (COLUMNS, 2 * runs * rows, width)
     return own.reshape(shape), swap(own, CORE).reshape(shape), token

time: 239 us -> 235 us (0.983)
  Pallas kernels: 136 us -> 132 us
    pallas_call x34, Pallas kernels: 136 us -> 132 us  [call(): pl.pallas_call(run, grid_spec=pltpu.PrefetchScalarGridSpec(num_scalar_pre...]
  transfers between devices with their start and end apart: 49 -> 49, of which waited for: 20 -> 18; matrix products, arithmetic and copies ran while one was open for 0% -> 1% of each run, Pallas kernels for 48% -> 49%
where the time goes in v3:
time: 235 us
  Pallas kernels  132 us (56%)
  starting transfers between devices  58.2 us (25%)
  waiting for transfers between devices  39.8 us (17%)
  local copies, waits for them, and re-layouts  3.87 us (2%)
    pallas_call x34, Pallas kernels, call(): pl.pallas_call(run, grid_spec=pltpu.PrefetchScalarGridSpec(num_scalar_pre...  132 us
    ppermute x49, starting transfers between devices, swap(): return lax.ppermute(v, AXES, [(i, i ^ mask) for i in range(32)])  58.2 us
    ppermute x49, waiting for transfers between devices, swap(): return lax.ppermute(v, AXES, [(i, i ^ mask) for i in range(32)])  39.8 us
  transfers between devices with their start and end apart: 49, of which 18 were waited for; matrix products, arithmetic and copies ran while one was open for 1% of the time, Pallas kernels for 49%

profile of v3, /device:TPU:0, one launch (start us, length us, event | category | flops | bytes accessed | tf_op | source)
XLA Modules:
  0.0 234.6 jit_solution(2058070437178710373)
XLA Ops:
  2.3 3.0 %collective-permute-start = (bf16[24,3072]{1,0:T(8,128)(2,1)S(1)}, bf16[24,3072]{1,0:T(8,128)(2,1)S(1)}, u32[]{:S(2)}, u32[]{:S(2)}) collective-permute-start(bf16[24,3072]{1,0:T(8,128)(2,1)S(1)} %get-tuple-element.138.refs_1_), channel_id=1, source_target_pairs={{0,8},{1,9},{2,10},{3,11},{4,12},{5,13},{6,14},{7,15},{8,0},{9,1},... | collective-permute-start | bytes 442376 | tf_op jit(solution)/shard_map/ppermute | solution.py:398
  5.4 2.6 %collective-permute-start.1 = (bf16[24,3072]{1,0:T(8,128)(2,1)S(1)}, bf16[24,3072]{1,0:T(8,128)(2,1)S(1)}, u32[]{:S(2)}, u32[]{:S(2)}) collective-permute-start(bf16[24,3072]{1,0:T(8,128)(2,1)S(1)} %get-tuple-element.138.refs_1_), channel_id=1, source_target_pairs={{0,16},{1,17},{2,18},{3,19},{4,20},{5,21},{6,22},{7,23},{8,24},{9,... | collective-permute-start | bytes 442376 | tf_op jit(solution)/shard_map/ppermute | solution.py:398
  14.0 5.3 %collective-permute-done.1.refs_3_ = bf16[24,3072]{1,0:T(8,128)(2,1)S(1)} collective-permute-done((bf16[24,3072]{1,0:T(8,128)(2,1)S(1)}, bf16[24,3072]{1,0:T(8,128)(2,1)S(1)}, u32[]{:S(2)}, u32[]{:S(2)}) %collective-permute-start.1) | collective-permute-done | bytes 147488 | tf_op jit(solution)/shard_map/ppermute | solution.py:398
  23.6 2.3 collective-permute-start.7
  25.9 2.5 %collective-permute-start.8 = (bf16[24,3072]{1,0:T(8,128)(2,1)S(1)}, bf16[24,3072]{1,0:T(8,128)(2,1)S(1)}, u32[]{:S(2)}, u32[]{:S(2)}) collective-permute-start(bf16[24,3072]{1,0:T(8,128)(2,1)S(1)} %get-tuple-element.143.refs_1_), channel_id=1, source_target_pairs={{0,24},{1,25},{2,26},{3,27},{4,28},{5,29},{6,30},{7,31},{8,16},{9,... | collective-permute-start | bytes 442376 | tf_op jit(solution)/shard_map/ppermute | solution.py:398
  30.3 3.2 %collective-permute-done.8.refs_6_.refs_4_ = bf16[24,3072]{1,0:T(8,128)(2,1)S(1)} collective-permute-done((bf16[24,3072]{1,0:T(8,128)(2,1)S(1)}, bf16[24,3072]{1,0:T(8,128)(2,1)S(1)}, u32[]{:S(2)}, u32[]{:S(2)}) %collective-permute-start.8) | collective-permute-done | bytes 147488 | tf_op jit(solution)/shard_map/ppermute | solution.py:398
  35.3 2.6 %collective-permute-start.11 = (bf16[24,3072]{1,0:T(8,128)(2,1)S(1)}, bf16[24,3072]{1,0:T(8,128)(2,1)S(1)}, u32[]{:S(2)}, u32[]{:S(2)}) collective-permute-start(bf16[24,3072]{1,0:T(8,128)(2,1)S(1)} %get-tuple-element.143.refs_1_), channel_id=1, source_target_pairs={{0,16},{1,17},{2,18},{3,19},{4,20},{5,21},{6,22},{7,23},{8,24},{9,... | collective-permute-start | bytes 442376 | tf_op jit(solution)/shard_map/ppermute | solution.py:398
  41.4 7.7 %shard_map.240 = (bf16[1024,768]{1,0:T(8,128)(2,1)}, bf16[1024,768]{1,0:T(8,128)(2,1)}, bf16[1024,768]{1,0:T(8,128)(2,1)}, bf16[1024,768]{1,0:T(8,128)(2,1)}, f3...) custom-call(s32[16]{0:T(128)S(1)} %reshape.65.refs_0_, bf16[1024,768]{1,0:T(8,128)(2,1)} %refs_1_.3, bf16[1024,768]{1,0:T(8,128)(2,1)} %refs_2_.3, ...), custom_call_target="tpu_custom_call" | custom-call | flops 1 | bytes 1 | tf_op jit(solution)/shard_map/pallas_call | solution.py:44
  55.1 10.5 %shard_map.243 = (bf16[1024,2304]{1,0:T(8,128)(2,1)}, bf16[1024,768]{1,0:T(8,128)(2,1)S(1)}, f32[96,128]{1,0:T(8,128)S(1)}, f32[8,128]{1,0:T(8,128)S(1)}) custom-call(s32[16]{0:T(128)S(1)} %reshape.65.refs_0_, s32[4]{0:T(128)S(1)} %pad_add_fusion.refs_0_.refs_1_, bf16[1024,768]{1,0:T(8,128)(2,1)} %get-tuple-element.145.refs_2_.refs_1_, ...), custom_call_target="tpu_custom_call" | custom-call | flops 1 | bytes 1 | tf_op jit(solution)/shard_map/pallas_call | solution.py:44
  72.1 4.3 %shard_map.245 = (f32[1024,768]{1,0:T(8,128)}, bf16[1024,768]{1,0:T(8,128)(2,1)S(1)}, f32[8,128]{1,0:T(8,128)S(1)}) custom-call(s32[4]{0:T(128)S(1)} %pad_add_fusion.refs_0_.refs_1_, bf16[1024,768]{1,0:T(8,128)(2,1)S(1)} %get-tuple-element.153.refs_1_.refs_2_, bf16[1024,768]{1,0:T(8,128)(2,1)S(1)} %copy-done, f32[2,768]{1,0:T(2,128)S(1)} %copy-done.8, ...), custom_call_target="tpu_custom_call" | custom-call | flops 1 | bytes 1 | tf_op jit(solution)/shard_map/pallas_call | solution.py:44
  76.4 4.2 %collective-permute-done.19.refs_4_ = bf16[2,2,24,1536]{3,2,1,0:T(8,128)(2,1)S(1)} collective-permute-done((bf16[2,2,24,1536]{3,2,1,0:T(8,128)(2,1)S(1)}, bf16[2,2,24,1536]{3,2,1,0:T(8,128)(2,1)S(1)}, u32[]{:S(2)}, u32[]{:S(2)}) %collective-permute-start.19) | collective-permute-done | bytes 294944 | tf_op jit(solution)/shard_map/ppermute | solution.py:398
  86.7 2.5 %collective-permute-done.20 = bf16[4,2,2,24,3072]{4,3,2,1,0:T(8,128)(2,1)S(1)} collective-permute-done((bf16[4,2,2,24,3072]{4,3,2,1,0:T(8,128)(2,1)S(1)}, bf16[4,2,2,24,3072]{4,3,2,1,0:T(8,128)(2,1)S(1)}, u32[]{:S(2)}, u32[]{:S(2)}) %collective-permute-start.20) | collective-permute-done | bytes 2359328 | tf_op jit(solution)/shard_map/ppermute | solution.py:398
  89.2 11.9 %shard_map.248 = (bf16[1024,3072]{1,0:T(8,128)(2,1)}, f32[1024,3072]{1,0:T(8,128)}, bf16[8,192,768]{2,1,0:T(8,128)(2,1)}, bf16[8,192,768]{2,1,0:T(8,128)(2,1)}, f32[8,128]{1,0:T(8,128)S(1)}) custom-call(s32[4]{0:T(128)S(1)} %pad_add_fusion.refs_0_.refs_1_, bf16[1024,768]{1,0:T(8,128)(2,1)S(1)} %get-tuple-element.159.refs_1_.refs_2_, ...), custom_call_target="tpu_custom_call" | custom-call | flops 1 | bytes 1 | tf_op jit(solution)/shard_map/pallas_call | solution.py:44
  102.1 5.1 %shard_map.250 = (bf16[1024,3072]{1,0:T(8,128)(2,1)}, f32[1024,3072]{1,0:T(8,128)}, bf16[8,192,768]{2,1,0:T(8,128)(2,1)}, bf16[8,192,768]{2,1,0:T(8,128)(2,1)}, f32[8,128]{1,0:T(8,128)}) custom-call(s32[4]{0:T(128)S(1)} %pad_add_fusion.refs_0_.refs_1_, ...), custom_call_target="tpu_custom_call", output_to_operand_aliasing={{0}: (6, {}), {1}: (7, {}), {2}: (8, {}), {3}: (9, {})} | custom-call | flops 1 | bytes 1 | tf_op jit(solution)/shard_map/pallas_call | solution.py:44
  107.6 15.7 %shard_map.251 = (bf16[1024,3072]{1,0:T(8,128)(2,1)}, f32[1,3072]{1,0:T(1,128)S(1)}, bf16[8,48,3072]{2,1,0:T(8,128)(2,1)}, bf16[8,48,3072]{2,1,0:T(8,128)(2,1)}, f32[8,128]{1,0:T(8,128)S(1)}) custom-call(s32[4]{0:T(128)S(1)} %pad_add_fusion.refs_0_.refs_1_, bf16[1024,768]{1,0:T(8,128)(2,1)} %get-tuple-element.160.refs_2_.refs_1_, ...), custom_call_target="tpu_custom_call" | custom-call | flops 1 | bytes 1 | tf_op jit(solution)/shard_map/pallas_call | solution.py:44
  127.1 14.8 %shard_map.253 = (f32[1024,768]{1,0:T(8,128)}, bf16[1024,768]{1,0:T(8,128)(2,1)S(1)}, bf16[1024,768]{1,0:T(8,128)(2,1)S(1)}, f32[4,768]{1,0:T(4,128)S(1)}, f32[8,128]{1,0:T(8,128)S(1)}) custom-call(s32[4]{0:T(128)S(1)} %pad_add_fusion.refs_0_.refs_1_, bf16[1024,3072]{1,0:T(8,128)(2,1)} %get-tuple-element.182.refs_1_, bf16[8,48,3072]{2,1,0:T(8,128)(2,1)S(1)} %bitcast.27, ...), custom_call_target="tpu_custom_call" | custom-call | flops 1 | bytes 1 | tf_op jit(solution)/shard_map/pallas_call | solution.py:44
  144.9 12.8 %shard_map.255 = (bf16[1024,2304]{1,0:T(8,128)(2,1)S(1)}, f32[8,2304]{1,0:T(8,128)S(1)}, f32[8,128]{1,0:T(8,128)S(1)}) custom-call(s32[16]{0:T(128)S(1)} %reshape.65.refs_0_, bf16[1024,2304]{1,0:T(8,128)(2,1)} %get-tuple-element.196.refs_1_, bf16[1024,768]{1,0:T(8,128)(2,1)S(1)} %get-tuple-element.197.refs_2_, f32[96,128]{1,0:T(8,128)S(1)} %get-tuple-element.198.refs_3_, ...), custom_call_target="tpu_custom_call" | custom-call | flops 1 | bytes 1 | tf_op jit(solution)/shard_map/pallas_call | solution.py:44
  160.5 7.3 %shard_map.257 = (bf16[8,48,3072]{2,1,0:T(8,128)(2,1)S(1)}, bf16[8,48,3072]{2,1,0:T(8,128)(2,1)S(1)}, f32[8,128]{1,0:T(8,128)S(1)}) custom-call(s32[4]{0:T(128)S(1)} %pad_add_fusion.refs_0_.refs_1_, bf16[1024,768]{1,0:T(8,128)(2,1)S(1)} %copy-done.5, bf16[1024,768]{1,0:T(8,128)(2,1)S(1)} %get-tuple-element.153.refs_1_.refs_2_, ...), custom_call_target="tpu_custom_call" | custom-call | flops 1 | bytes 1 | tf_op jit(solution)/shard_map/pallas_call | solution.py:44
  169.6 11.2 %shard_map.258 = (f32[1024,768]{1,0:T(8,128)}, f32[2,768]{1,0:T(2,128)S(1)}, f32[8,128]{1,0:T(8,128)S(1)}) custom-call(s32[16]{0:T(128)S(1)} %reshape.65.refs_0_, s32[4]{0:T(128)S(1)} %pad_add_fusion.refs_0_.refs_1_, bf16[1024,2304]{1,0:T(8,128)(2,1)S(1)} %get-tuple-element.205.refs_3_.refs_2_, bf16[8,48,3072]{2,1,0:T(8,128)(2,1)S(1)} %bitcast.20, ...), custom_call_target="tpu_custom_call" | custom-call | flops 1 | bytes 1 | tf_op jit(solution)/shard_map/pallas_call | solution.py:44
  189.7 11.2 %shard_map.261 = (bf16[1024,768]{1,0:T(8,128)(2,1)}, f32[1,768]{1,0:T(1,128)S(1)}, f32[8,128]{1,0:T(8,128)S(1)}) custom-call(s32[16]{0:T(128)S(1)} %reshape.65.refs_0_, s32[4]{0:T(128)S(1)} %pad_add_fusion.refs_0_.refs_1_, bf16[1024,3072]{1,0:T(8,128)(2,1)} %get-tuple-element.175.refs_2_, bf16[8,192,768]{2,1,0:T(8,128)(2,1)S(1)} %bitcast.32, ...), custom_call_target="tpu_custom_call" | custom-call | flops 1 | bytes 1 | tf_op jit(solution)/shard_map/pallas_call | solution.py:44
  206.7 4.2 %collective-permute-done.39.refs_2_ = f32[14,768]{1,0:T(8,128)S(1)} collective-permute-done((f32[14,768]{1,0:T(8,128)S(1)}, f32[14,768]{1,0:T(8,128)S(1)}, u32[]{:S(2)}, u32[]{:S(2)}) %collective-permute-start.39) | collective-permute-done | bytes 43040 | tf_op jit(solution)/shard_map/ppermute | solution.py:398
  212.2 2.7 %collective-permute-start.42 = (bf16[24,3072]{1,0:T(8,128)(2,1)S(1)}, bf16[24,3072]{1,0:T(8,128)(2,1)S(1)}, u32[]{:S(2)}, u32[]{:S(2)}) collective-permute-start(bf16[24,3072]{1,0:T(8,128)(2,1)S(1)} %get-tuple-element.242), channel_id=1, source_target_pairs={{0,8},{1,9},{2,10},{3,11},{4,12},{5,13},{6,14},{7,15},{8,0},{9,1},... | collective-permute-start | bytes 442376 | tf_op jit(solution)/shard_map/ppermute | solution.py:398
  218.4 3.0 %collective-permute-done.45.refs_2_ = f32[14,768]{1,0:T(8,128)S(1)} collective-permute-done((f32[14,768]{1,0:T(8,128)S(1)}, f32[14,768]{1,0:T(8,128)S(1)}, u32[]{:S(2)}, u32[]{:S(2)}) %collective-permute-start.45) | collective-permute-done | bytes 43040 | tf_op jit(solution)/shard_map/ppermute | solution.py:398
  227.7 5.0 %collective-permute-done.47.refs_3_ = f32[14,768]{1,0:T(8,128)S(1)} collective-permute-done((f32[14,768]{1,0:T(8,128)S(1)}, f32[14,768]{1,0:T(8,128)S(1)}, u32[]{:S(2)}, u32[]{:S(2)}) %collective-permute-start.47) | collective-permute-done | bytes 43040 | tf_op jit(solution)/shard_map/ppermute | solution.py:398
  (161 shorter events, 77.9 us)
Async XLA Ops:
  34.2 15.6 %collective-permute-start.10 = (bf16[2,4,24,1536]{3,2,1,0:T(8,128)(2,1)S(1)}, bf16[2,4,24,1536]{3,2,1,0:T(8,128)(2,1)S(1)}, u32[]{:S(2)}, u32[]{:S(2)}) collective-permute-start(bf16[2,4,24,1536]{3,2,1,0:T(8,128)(2,1)S(1)} %get-tuple-element.147.refs_3_), channel_id=1, source_target_pairs={{0,4},{1,5},{2,6},{3,7},{4,0},{5,1},{6,2},{7,3},{8,12},{9,13},{10,... | collective-permute-start | bytes 1769480 | tf_op jit(solution)/shard_map/ppermute | solution.py:398
  34.8 15.0 %collective-permute-start.9 = (bf16[2,4,24,1536]{3,2,1,0:T(8,128)(2,1)S(1)}, bf16[2,4,24,1536]{3,2,1,0:T(8,128)(2,1)S(1)}, u32[]{:S(2)}, u32[]{:S(2)}) collective-permute-start(bf16[2,4,24,1536]{3,2,1,0:T(8,128)(2,1)S(1)} %get-tuple-element.146.refs_1_), channel_id=1, source_target_pairs={{0,1},{1,0},{2,3},{3,2},{4,5},{5,4},{6,7},{7,6},{8,9},{9,8},{10,11... | collective-permute-start | bytes 1769480 | tf_op jit(solution)/shard_map/ppermute | solution.py:398
  50.5 16.1 %collective-permute-start.16 = (bf16[2,2,24,1536]{3,2,1,0:T(8,128)(2,1)S(1)}, bf16[2,2,24,1536]{3,2,1,0:T(8,128)(2,1)S(1)}, u32[]{:S(2)}, u32[]{:S(2)}) collective-permute-start(bf16[2,2,24,1536]{3,2,1,0:T(8,128)(2,1)S(1)} %get-tuple-element.149.refs_1_), channel_id=1, source_target_pairs={{0,16},{1,17},{2,18},{3,19},{4,20},{5,21},{6,22},{7,23},{8,24},{9,... | collective-permute-start | bytes 884744 | tf_op jit(solution)/shard_map/ppermute | solution.py:398
  50.9 15.7 %collective-permute-start.14 = (bf16[4,24,1536]{2,1,0:T(8,128)(2,1)S(1)}, bf16[4,24,1536]{2,1,0:T(8,128)(2,1)S(1)}, u32[]{:S(2)}, u32[]{:S(2)}) collective-permute-start(bf16[4,24,1536]{2,1,0:T(8,128)(2,1)S(1)} %get-tuple-element.155.refs_1_), channel_id=1, source_target_pairs={{0,4},{1,5},{2,6},{3,7},{4,0},{5,1},{6,2},{7,3},{8,12},{9,13},{10,... | collective-permute-start | bytes 884744 | tf_op jit(solution)/shard_map/ppermute | solution.py:398
  52.4 14.2 %collective-permute-start.15 = (bf16[4,24,1536]{2,1,0:T(8,128)(2,1)S(1)}, bf16[4,24,1536]{2,1,0:T(8,128)(2,1)S(1)}, u32[]{:S(2)}, u32[]{:S(2)}) collective-permute-start(bf16[4,24,1536]{2,1,0:T(8,128)(2,1)S(1)} %get-tuple-element.156.refs_3_), channel_id=1, source_target_pairs={{0,1},{1,0},{2,3},{3,2},{4,5},{5,4},{6,7},{7,6},{8,9},{9,8},{10,11... | collective-permute-start | bytes 884744 | tf_op jit(solution)/shard_map/ppermute | solution.py:398
  67.3 15.4 %collective-permute-start.17 = (bf16[2,4,24,1536]{3,2,1,0:T(8,128)(2,1)S(1)}, bf16[2,4,24,1536]{3,2,1,0:T(8,128)(2,1)S(1)}, u32[]{:S(2)}, u32[]{:S(2)}) collective-permute-start(bf16[2,4,24,1536]{3,2,1,0:T(8,128)(2,1)S(1)} %get-tuple-element.161.refs_1_), channel_id=1, source_target_pairs={{0,1},{1,0},{2,3},{3,2},{4,5},{5,4},{6,7},{7,6},{8,9},{9,8},{10,11... | collective-permute-start | bytes 1769480 | tf_op jit(solution)/shard_map/ppermute | solution.py:398
  68.8 15.0 %collective-permute-start.18 = (bf16[2,4,24,1536]{3,2,1,0:T(8,128)(2,1)S(1)}, bf16[2,4,24,1536]{3,2,1,0:T(8,128)(2,1)S(1)}, u32[]{:S(2)}, u32[]{:S(2)}) collective-permute-start(bf16[2,4,24,1536]{3,2,1,0:T(8,128)(2,1)S(1)} %get-tuple-element.162.refs_3_), channel_id=1, source_target_pairs={{0,4},{1,5},{2,6},{3,7},{4,0},{5,1},{6,2},{7,3},{8,12},{9,13},{10,... | collective-permute-start | bytes 1769480 | tf_op jit(solution)/shard_map/ppermute | solution.py:398
  84.7 16.5 %collective-permute-start.21 = (bf16[2,4,24,1536]{3,2,1,0:T(8,128)(2,1)S(1)}, bf16[2,4,24,1536]{3,2,1,0:T(8,128)(2,1)S(1)}, u32[]{:S(2)}, u32[]{:S(2)}) collective-permute-start(bf16[2,4,24,1536]{3,2,1,0:T(8,128)(2,1)S(1)} %get-tuple-element.171.refs_1_), channel_id=1, source_target_pairs={{0,1},{1,0},{2,3},{3,2},{4,5},{5,4},{6,7},{7,6},{8,9},{9,8},{10,11... | collective-permute-start | bytes 1769480 | tf_op jit(solution)/shard_map/ppermute | solution.py:398
  85.2 15.9 %collective-permute-start.22 = (bf16[2,4,24,1536]{3,2,1,0:T(8,128)(2,1)S(1)}, bf16[2,4,24,1536]{3,2,1,0:T(8,128)(2,1)S(1)}, u32[]{:S(2)}, u32[]{:S(2)}) collective-permute-start(bf16[2,4,24,1536]{3,2,1,0:T(8,128)(2,1)S(1)} %get-tuple-element.172.refs_3_), channel_id=1, source_target_pairs={{0,4},{1,5},{2,6},{3,7},{4,0},{5,1},{6,2},{7,3},{8,12},{9,13},{10,... | collective-permute-start | bytes 1769480 | tf_op jit(solution)/shard_map/ppermute | solution.py:398
  107.2 16.3 %collective-permute-start.25 = (bf16[8,192,768]{2,1,0:T(8,128)(2,1)}, bf16[8,192,768]{2,1,0:T(8,128)(2,1)S(1)}, u32[]{:S(2)}, u32[]{:S(2)}) collective-permute-start(bf16[8,192,768]{2,1,0:T(8,128)(2,1)} %get-tuple-element.184), channel_id=1, source_target_pairs={{0,2},{1,3},{2,0},{3,1},{4,6},{5,7},{6,4},{7,5},{8,10},{9,11},{10,... | collective-permute-start | bytes 7077896 | tf_op jit(solution)/shard_map/ppermute | solution.py:398
  123.3 18.6 %collective-permute-start.24 = (bf16[8,48,3072]{2,1,0:T(8,128)(2,1)}, bf16[8,48,3072]{2,1,0:T(8,128)(2,1)S(1)}, u32[]{:S(2)}, u32[]{:S(2)}) collective-permute-start(bf16[8,48,3072]{2,1,0:T(8,128)(2,1)} %get-tuple-element.181), channel_id=1, source_target_pairs={{0,2},{1,3},{2,0},{3,1},{4,6},{5,7},{6,4},{7,5},{8,10},{9,11},{10,... | collective-permute-start | bytes 7077896 | tf_op jit(solution)/shard_map/ppermute | solution.py:398
  124.7 33.0 %collective-permute-start.27 = (bf16[4,2,96,384]{3,2,1,0:T(8,128)(2,1)S(1)}, bf16[4,2,96,384]{3,2,1,0:T(8,128)(2,1)S(1)}, u32[]{:S(2)}, u32[]{:S(2)}) collective-permute-start(bf16[4,2,96,384]{3,2,1,0:T(8,128)(2,1)S(1)} %get-tuple-element.191), channel_id=1, source_target_pairs={{0,1},{1,0},{2,3},{3,2},{4,5},{5,4},{6,7},{7,6},{8,9},{9,8},{10,11... | collective-permute-start | bytes 1769480 | tf_op jit(solution)/shard_map/ppermute | solution.py:398
  125.6 32.0 %collective-permute-start.29 = (bf16[4,2,96,384]{3,2,1,0:T(8,128)(2,1)S(1)}, bf16[4,2,96,384]{3,2,1,0:T(8,128)(2,1)S(1)}, u32[]{:S(2)}, u32[]{:S(2)}) collective-permute-start(bf16[4,2,96,384]{3,2,1,0:T(8,128)(2,1)S(1)} %get-tuple-element.195), channel_id=1, source_target_pairs={{0,4},{1,5},{2,6},{3,7},{4,0},{5,1},{6,2},{7,3},{8,12},{9,13},{10,... | collective-permute-start | bytes 1769480 | tf_op jit(solution)/shard_map/ppermute | solution.py:398
  143.1 15.2 %collective-permute-start.26 = (bf16[4,2,24,1536]{3,2,1,0:T(8,128)(2,1)S(1)}, bf16[4,2,24,1536]{3,2,1,0:T(8,128)(2,1)S(1)}, u32[]{:S(2)}, u32[]{:S(2)}) collective-permute-start(bf16[4,2,24,1536]{3,2,1,0:T(8,128)(2,1)S(1)} %get-tuple-element.189), channel_id=1, source_target_pairs={{0,1},{1,0},{2,3},{3,2},{4,5},{5,4},{6,7},{7,6},{8,9},{9,8},{10,11... | collective-permute-start | bytes 1769480 | tf_op jit(solution)/shard_map/ppermute | solution.py:398
  144.3 14.7 %collective-permute-start.28 = (bf16[4,2,24,1536]{3,2,1,0:T(8,128)(2,1)S(1)}, bf16[4,2,24,1536]{3,2,1,0:T(8,128)(2,1)S(1)}, u32[]{:S(2)}, u32[]{:S(2)}) collective-permute-start(bf16[4,2,24,1536]{3,2,1,0:T(8,128)(2,1)S(1)} %get-tuple-element.193), channel_id=1, source_target_pairs={{0,4},{1,5},{2,6},{3,7},{4,0},{5,1},{6,2},{7,3},{8,12},{9,13},{10,... | collective-permute-start | bytes 1769480 | tf_op jit(solution)/shard_map/ppermute | solution.py:398
  167.8 16.6 %collective-permute-start.30 = (bf16[4,24,3072]{2,1,0:T(8,128)(2,1)S(1)}, bf16[4,24,3072]{2,1,0:T(8,128)(2,1)S(1)}, u32[]{:S(2)}, u32[]{:S(2)}) collective-permute-start(bf16[4,24,3072]{2,1,0:T(8,128)(2,1)S(1)} %get-tuple-element.202), channel_id=1, source_target_pairs={{0,4},{1,5},{2,6},{3,7},{4,0},{5,1},{6,2},{7,3},{8,12},{9,13},{10,... | collective-permute-start | bytes 1769480 | tf_op jit(solution)/shard_map/ppermute | solution.py:398
  168.5 15.9 %collective-permute-start.31 = (bf16[4,24,3072]{2,1,0:T(8,128)(2,1)S(1)}, bf16[4,24,3072]{2,1,0:T(8,128)(2,1)S(1)}, u32[]{:S(2)}, u32[]{:S(2)}) collective-permute-start(bf16[4,24,3072]{2,1,0:T(8,128)(2,1)S(1)} %get-tuple-element.204), channel_id=1, source_target_pairs={{0,1},{1,0},{2,3},{3,2},{4,5},{5,4},{6,7},{7,6},{8,9},{9,8},{10,11... | collective-permute-start | bytes 1769480 | tf_op jit(solution)/shard_map/ppermute | solution.py:398
  182.0 18.9 %collective-permute-start.33 = (bf16[4,2,24,1536]{3,2,1,0:T(8,128)(2,1)S(1)}, bf16[4,2,24,1536]{3,2,1,0:T(8,128)(2,1)S(1)}, u32[]{:S(2)}, u32[]{:S(2)}) collective-permute-start(bf16[4,2,24,1536]{3,2,1,0:T(8,128)(2,1)S(1)} %get-tuple-element.218), channel_id=1, source_target_pairs={{0,1},{1,0},{2,3},{3,2},{4,5},{5,4},{6,7},{7,6},{8,9},{9,8},{10,11... | collective-permute-start | bytes 1769480 | tf_op jit(solution)/shard_map/ppermute | solution.py:398
  183.1 17.9 %collective-permute-start.34 = (bf16[4,2,24,1536]{3,2,1,0:T(8,128)(2,1)S(1)}, bf16[4,2,24,1536]{3,2,1,0:T(8,128)(2,1)S(1)}, u32[]{:S(2)}, u32[]{:S(2)}) collective-permute-start(bf16[4,2,24,1536]{3,2,1,0:T(8,128)(2,1)S(1)} %get-tuple-element.220), channel_id=1, source_target_pairs={{0,4},{1,5},{2,6},{3,7},{4,0},{5,1},{6,2},{7,3},{8,12},{9,13},{10,... | collective-permute-start | bytes 1769480 | tf_op jit(solution)/shard_map/ppermute | solution.py:398
  185.3 15.6 %collective-permute-start.35 = (bf16[24,6144]{1,0:T(8,128)(2,1)S(1)}, bf16[24,6144]{1,0:T(8,128)(2,1)S(1)}, u32[]{:S(2)}, u32[]{:S(2)}) collective-permute-start(bf16[24,6144]{1,0:T(8,128)(2,1)S(1)} %get-tuple-element.222), channel_id=1, source_target_pairs={{0,8},{1,9},{2,10},{3,11},{4,12},{5,13},{6,14},{7,15},{8,0},{9,1},... | collective-permute-start | bytes 884744 | tf_op jit(solution)/shard_map/ppermute | solution.py:398
  185.7 25.8 %collective-permute-start.40 = (bf16[24,6144]{1,0:T(8,128)(2,1)S(1)}, bf16[24,6144]{1,0:T(8,128)(2,1)S(1)}, u32[]{:S(2)}, u32[]{:S(2)}) collective-permute-start(bf16[24,6144]{1,0:T(8,128)(2,1)S(1)} %get-tuple-element.239), channel_id=1, source_target_pairs={{0,16},{1,17},{2,18},{3,19},{4,20},{5,21},{6,22},{7,23},{8,24},{9,... | collective-permute-start | bytes 884744 | tf_op jit(solution)/shard_map/ppermute | solution.py:398
  187.7 23.8 %collective-permute-start.41 = (bf16[24,6144]{1,0:T(8,128)(2,1)S(1)}, bf16[24,6144]{1,0:T(8,128)(2,1)S(1)}, u32[]{:S(2)}, u32[]{:S(2)}) collective-permute-start(bf16[24,6144]{1,0:T(8,128)(2,1)S(1)} %get-tuple-element.240), channel_id=1, source_target_pairs={{0,24},{1,25},{2,26},{3,27},{4,28},{5,29},{6,30},{7,31},{8,16},{9,... | collective-permute-start | bytes 884744 | tf_op jit(solution)/shard_map/ppermute | solution.py:398
  214.9 17.8 %collective-permute-start.43 = (bf16[24,3072]{1,0:T(8,128)(2,1)S(1)}, bf16[24,3072]{1,0:T(8,128)(2,1)S(1)}, u32[]{:S(2)}, u32[]{:S(2)}) collective-permute-start(bf16[24,3072]{1,0:T(8,128)(2,1)S(1)} %get-tuple-element.243), channel_id=1, source_target_pairs={{0,16},{1,17},{2,18},{3,19},{4,20},{5,21},{6,22},{7,23},{8,24},{9,... | collective-permute-start | bytes 442376 | tf_op jit(solution)/shard_map/ppermute | solution.py:398
  215.4 17.3 %collective-permute-start.44 = (bf16[24,3072]{1,0:T(8,128)(2,1)S(1)}, bf16[24,3072]{1,0:T(8,128)(2,1)S(1)}, u32[]{:S(2)}, u32[]{:S(2)}) collective-permute-start(bf16[24,3072]{1,0:T(8,128)(2,1)S(1)} %get-tuple-element.244), channel_id=1, source_target_pairs={{0,24},{1,25},{2,26},{3,27},{4,28},{5,29},{6,30},{7,31},{8,16},{9,... | collective-permute-start | bytes 442376 | tf_op jit(solution)/shard_map/ppermute | solution.py:398
  (47 other events, 470.7 us)
